TPU v7x, 32 devices: a whole 2x2x4 slice. The times are simulated.
32 devices in a mesh: rad: 16 (over z, y, x), lat: 2 (over core).
Axes of the slice: x: 2, y: 2, z: 4, core: 2. Of those that a mesh axis runs over, the one named last changes fastest.
Arguments:
- forcing: float32 [3, 2, 5120, 64], P(None, None, ('rad', 'lat')), may hold values from -6 to 6
- pivots: float32 [5120, 2, 32, 32], P(('rad', 'lat')), may hold values from -1 to 2
- lower: float32 [5120, 1, 32, 32], P(('rad', 'lat')), may hold values from -1 to 2
- upper: float32 [5120, 1, 32, 32], P(('rad', 'lat')), may hold values from -1 to 1.5
- slab_modes: int32 [5], replicated, may hold values from 0 to 511, as said below
- slot_of_column: int32 [5120], replicated, may hold values from 0 to 5119, each once
- legendre: bfloat16 [5, 1024, 768], P(None, None, 'lat'), may hold values from -0.1875 to 0.1875
- cycle_weight: float32 [768], P('lat'), may hold values from 0.5 to 2
- zonal_flow: bfloat16 [64, 768, 1536], P('rad', 'lat'), may hold values from -12 to 12
- inverse_spacing: float32 [64], replicated, may hold values from 0.03 to 0.3
Outputs:
- solved: float32 [3, 2, 5120, 64], P(None, None, ('rad', 'lat'))
- explicit_term: float32 [3, 2, 5120, 64], P(None, None, ('rad', 'lat'))
Inputs may be any that keep to these rules, and one draw needn't show every extreme that they name: `slab_modes`: 5 distinct wave numbers below 512, one of them 1024 // 2 - 1. `slot_of_column`: every slot number appears once.
All inputs are finite; a program needn't handle non-finite values.
Results may differ from a plain program's by a relative error of at most 0.0051.
Values may be sent and summed in bfloat16 or wider, within the bound.
A program may use at most 128 MiB of HBM per device.

v0:
```python
import math

import jax
import jax.numpy as jnp
from jax import lax
from jax.sharding import PartitionSpec as P


def with_halo(value, sides, width):
    for axis, dim in sides:
        peers, length = (lax.axis_size(axis), value.shape[dim])
        up = [(i, (i + 1) % peers) for i in range(peers - 1)]
        down = [(j, i) for i, j in up]
        last = lax.slice_in_dim(value, length - width, length, axis=dim)
        initial = lax.slice_in_dim(value, 0, width, axis=dim)
        before = lax.ppermute(last, axis, up)
        after = lax.ppermute(initial, axis, down)
        value = jnp.concatenate([before, value, after], axis=dim)
    return value


def radial_solve(forcing, pivots, lower, upper):
    slot_count = forcing.shape[2]
    block_count = pivots.shape[1]
    block_size = pivots.shape[2]
    highest = lax.Precision.HIGHEST
    blocks = jnp.moveaxis(forcing.reshape(3, 2, slot_count, block_count, block_size), 3, 0)

    def apply_block(matrix, vector):
        return jnp.einsum("kij,fckj->fcki", matrix, vector, precision=highest)

    leading = apply_block(pivots[:, 0], blocks[0])

    def descend(carry, element):
        pivot_block, lower_block, rhs_block = element
        advanced = apply_block(pivot_block, rhs_block - apply_block(lower_block, carry))
        return (advanced, advanced)

    _, trailing = lax.scan(
        descend, leading, (jnp.moveaxis(pivots[:, 1:], 1, 0), jnp.moveaxis(lower, 1, 0), blocks[1:])
    )
    forward = jnp.concatenate([leading[None], trailing], 0)
    final_block = forward[-1]

    def up_step(carry, element):
        upper_block, forward_block = element
        current = forward_block - apply_block(upper_block, carry)
        return (current, current)

    _, earlier = lax.scan(
        up_step, final_block, (jnp.moveaxis(upper, 1, 0), forward[:-1]), reverse=True
    )
    result = jnp.concatenate([earlier, final_block[None]], 0)
    return jnp.moveaxis(result, 0, 3).reshape(3, 2, slot_count, block_count * block_size)


def phi_tables(slab_modes, phi_count, degree_count):
    columns = jnp.arange(phi_count, dtype=jnp.int32)
    residues = slab_modes[:, None] * columns[None, :] % phi_count
    angles = residues.astype(jnp.float32) * (2.0 * math.pi / phi_count)
    factor = slab_modes.astype(jnp.float32)[:, None] * (2.0 / degree_count)
    slope_table = jnp.concatenate([-factor * jnp.sin(angles), -factor * jnp.cos(angles)], 0).astype(
        jnp.bfloat16
    )
    back_table = (
        jnp.concatenate([jnp.cos(angles), -jnp.sin(angles)], 0) * (2.0 / phi_count)
    ).astype(jnp.bfloat16)
    return (slope_table, back_table)


def level_stencil(padded, center, spacing):
    width = center.shape[2]
    differences = (
        padded[:, :, 0:width]
        - 8.0 * padded[:, :, 1 : width + 1]
        + 8.0 * padded[:, :, 3 : width + 3]
        - padded[:, :, 4 : width + 4]
    )
    return center + spacing[None, None, :, None] * differences


def body(
    forcing,
    pivots,
    lower,
    upper,
    slab_modes,
    slot_of_column,
    legendre,
    cycle_weight,
    zonal_flow,
    inverse_spacing,
):
    solved = radial_solve(forcing, pivots, lower, upper)
    per_device = forcing.shape[2]
    rad_count = lax.axis_size("rad")
    lat_count = lax.axis_size("lat")
    slot_count = per_device * rad_count * lat_count
    mode_count = legendre.shape[0]
    degree_count = legendre.shape[1]
    levels = zonal_flow.shape[0]
    cycle_count = zonal_flow.shape[1]
    phi_count = zonal_flow.shape[2]
    positions = jnp.arange(slot_count, dtype=jnp.int32)
    per_lat = per_device * rad_count
    lat_part = positions // per_lat
    remain = positions % per_lat
    column = (remain // per_device * lat_count + lat_part) * per_device + remain % per_device
    slot_at = jnp.take(slot_of_column, column)
    pos_of_slot = jnp.zeros((slot_count,), jnp.int32).at[slot_at].set(positions)
    allowed = jnp.arange(degree_count, dtype=jnp.int32)[None, :] >= slab_modes[:, None]
    slope_table, back_table = phi_tables(slab_modes, phi_count, degree_count)
    zonal_rows = zonal_flow.reshape(levels * cycle_count, phi_count)
    level_major = jnp.swapaxes(solved.astype(jnp.bfloat16), 2, 3)
    gathered = lax.all_gather(
        lax.all_to_all(level_major, "rad", split_axis=2, concat_axis=3, tiled=True),
        "lat",
        axis=3,
        tiled=True,
    )
    item_count = gathered.shape[0]
    coeffs = jnp.take(gathered, pos_of_slot, axis=3).reshape(
        item_count, 2, levels, mode_count, degree_count
    )
    coeffs = coeffs * allowed.astype(jnp.bfloat16)[None, None, None, :, :]
    spectral = jnp.einsum("fcrml,mlt->frtcm", coeffs, legendre, preferred_element_type=jnp.float32)
    spectral = spectral.astype(jnp.bfloat16).reshape(
        item_count, levels * cycle_count, 2 * mode_count
    )
    gradient = jnp.einsum("fak,kp->fap", spectral, slope_table, preferred_element_type=jnp.float32)
    product = (gradient * zonal_rows[None]).astype(jnp.bfloat16)
    modal = jnp.einsum("fap,kp->fak", product, back_table, preferred_element_type=jnp.float32)
    modal = modal.reshape(item_count, levels, cycle_count, 2, mode_count)
    weighted = (modal * cycle_weight[None, None, :, None, None]).astype(jnp.bfloat16)
    partial_value = jnp.einsum(
        "frtcm,mlt->fcrml", weighted, legendre, preferred_element_type=jnp.float32
    )
    partial_value = partial_value * allowed.astype(jnp.float32)[None, None, None, :, :]
    partial_value = jnp.take(
        partial_value.reshape(item_count, 2, levels, slot_count), slot_at, axis=3
    )
    half_slots = slot_count // lat_count
    summed = lax.psum(partial_value, "lat")
    share = lax.dynamic_slice_in_dim(summed, lax.axis_index("lat") * half_slots, half_slots, 3)
    spacing = lax.dynamic_slice_in_dim(inverse_spacing, lax.axis_index("rad") * levels, levels, 0)
    padded = with_halo(share, (("rad", 2),), 2)
    explicit_part = level_stencil(padded, share, spacing)
    explicit_levels = lax.all_to_all(explicit_part, "rad", split_axis=3, concat_axis=2, tiled=True)
    explicit_term = jnp.swapaxes(explicit_levels, 2, 3)
    return (solved, explicit_term)


def solution(mesh):
    placed = (
        P(None, None, ("rad", "lat"), None),
        P(("rad", "lat"), None, None, None),
        P(("rad", "lat"), None, None, None),
        P(("rad", "lat"), None, None, None),
        P(),
        P(),
        P(None, None, "lat"),
        P("lat"),
        P("rad", "lat", None),
        P(),
    )
    return jax.shard_map(
        body,
        mesh=mesh,
        in_specs=placed,
        out_specs=(P(None, None, ("rad", "lat"), None), P(None, None, ("rad", "lat"), None)),
        check_vma=False,
    )
```

profile of v0, /device:TPU:0, one launch (start us, length us, event | category | flops | bytes accessed | tf_op | source)
XLA Modules:
  0.0 415.8 jit_solution(8813550482866000583)
XLA Ops:
  7.2 2.6 copy.170
  9.7 3.1 fusion.87
  12.9 2.5 copy.210
  15.4 3.3 copy.209
  18.7 3.3 copy.193
  21.9 3.7 copy.195
  25.7 6.3 %fusion.9 = f32[3,2,160,32]{3,0,1,2:T(4,128)S(1)} fusion(f32[160,1,32,32]{3,2,0,1:T(8,128)} %copy.209, f32[2,3,2,160,32]{4,1,2,3,0:T(4,128)} %bitcast.120), kind=kOutput, calls=%fused_computation.16 | convolution fusion | flops 11796480 | bytes 3399680 | tf_op jit(solution)/shard_map/kij,fckj->fcki/dot_general | solution.py:30
  32.0 4.3 %fusion.12 = f32[3,2,160,32]{3,0,1,2:T(4,128)S(1)} fusion(f32[3,2,160,32]{3,0,1,2:T(4,128)S(1)} %fusion.9, f32[160,32,32,1]{2,1,3,0:T(8,128)S(1)} %copy-done.3, f32[2,3,2,160,32]{4,1,2,3,0:T(4,128)S(1)} %bitcast.121), kind=kOutput, calls=%fused_computation.19 | convolution fusion | flops 11827200 | bytes 1024000 | tf_op jit(solution)/shard_map/while/body/eval_jaxpr/kij,fckj->fcki/dot_general | solution.py:30
  36.3 4.2 %fusion.5 = f32[160,3,2,32]{3,1,2,0:T(4,128)S(1)} fusion(f32[3,2,160,32]{3,0,1,2:T(4,128)S(1)} %fusion.12, f32[160,1,32,32]{3,2,0,1:T(8,128)S(1)} %copy.210), kind=kOutput, calls=%fused_computation.11 | convolution fusion | flops 11796480 | bytes 901120 | tf_op jit(solution)/shard_map/while/body/eval_jaxpr/kij,fckj->fcki/dot_general | solution.py:30
  40.5 4.5 %fusion.14 = f32[1,3,2,160,32]{4,1,2,3,0:T(4,128)S(1)} fusion(f32[3,2,160,32]{3,0,1,2:T(4,128)S(1)} %fusion.9, f32[160,32,32,1]{2,1,3,0:T(8,128)S(1)} %copy-done.2, f32[160,3,2,32]{3,1,2,0:T(4,128)S(1)} %fusion.5), kind=kOutput, calls=%fused_computation.21 | convolution fusion | flops 11827200 | bytes 1024000 | tf_op jit(solution)/shard_map/while/body/eval_jaxpr/kij,fckj->fcki/dot_general | solution.py:30
  45.0 0.3 maximum_bitcast_fusion
  45.3 0.6 copy.175
  46.0 0.9 copy.176
  46.9 8.3 %all-to-all-start = ((bf16[3,2,64,160]{3,1,0,2:T(2,128)(2,1)}), bf16[3,2,64,160]{3,1,0,2:T(2,128)(2,1)S(1)}, u32[]{:S(2)}, u32[]{:S(2)}) async-start(bf16[3,2,64,160]{3,1,0,2:T(2,128)(2,1)} %copy.176), calls=%async_computation | async-start | bytes 393216 | tf_op jit(solution)/shard_map/all_to_all | solution.py:116
  55.2 0.3 compare_select_fusion.1
  55.5 28.7 %gather_fusion = s32[5120]{0:T(1024)S(1)} fusion(s32[5120]{0:T(1024)S(1)} %copy-done, s32[5120]{0:T(1024)S(1)} %broadcast_clamp_fusion.1), kind=kCustom, calls=%fused_computation | custom fusion | bytes 61440 | tf_op jit(solution)/shard_map/jit(_take)/gather | solution.py:109
  84.3 0.3 compare_select_fusion
  84.6 19.3 %scatter_custom_fusion = s32[5120]{0:T(1024)S(1)} fusion(s32[5120]{0:T(1024)S(1)} %bitcast.132, s32[5120]{0:T(1024)S(1)} %iota.30, s32[]{:T(128)} %constant.112.clone.1), kind=kCustom, calls=%fused_computation.120 | custom fusion | bytes 20484 | tf_op jit(solution)/shard_map/scatter | solution.py:110
  103.9 0.3 multiply_convert_fusion.2
  104.2 7.3 %bitcast_convert_fusion = f32[1536,1536]{1,0:T(8,128)} fusion(bf16[4,384,1536]{2,1,0:T(8,128)(2,1)} %param.18), kind=kLoop, calls=%fused_computation.6 | loop fusion | flops 2359296 | bytes 14155776 | tf_op jit(solution)/shard_map/convert_element_type | solution.py:131
  111.7 7.0 %copy.201 = bf16[3,2,4,16,160]{2,1,4,3,0:T(2,128)(2,1)} copy(bf16[3,2,4,16,160]{4,3,2,1,0:T(8,128)(2,1)S(1)} %bitcast.127) | data formatting | bytes 245760 | tf_op jit(solution)/shard_map/all_to_all | solution.py:116
  118.7 17.2 %all_gather.3 = bf16[3,2,4,5120]{2,1,3,0:T(2,128)(2,1)} all-gather(bf16[3,2,4,2560]{2,1,3,0:T(2,128)(2,1)} %bitcast.117), channel_id=1, replica_groups=mesh['rad'=16,'lat'=2] {'lat'}, dimensions={3}, use_global_device_ids=true | all-gather | bytes 368640 | tf_op jit(solution)/shard_map/all_gather | solution.py:115
  135.9 53.4 %gather_fusion.1 = bf16[5120,3,2,4]{3,2,1,0:T(2,128)(2,1)} fusion(bf16[3,2,4,5120]{2,1,3,0:T(2,128)(2,1)} %all_gather.3, s32[5120]{0:T(1024)S(1)} %fusion.80), kind=kCustom, calls=%fused_computation.1 | custom fusion | bytes 512000 | tf_op jit(solution)/shard_map/jit(_take)/gather | solution.py:122
  189.3 16.8 %copy.202 = bf16[3,2,4,5,1024]{4,3,2,1,0:T(8,128)(2,1)S(1)} copy(bf16[3,2,4,5,1024]{2,1,0,4,3:T(2,128)(2,1)} %bitcast.118) | data formatting | bytes 491520 | tf_op jit(solution)/shard_map/jit(_take)/gather | solution.py:122
  206.2 2.9 fusion.24
  209.2 11.1 %fusion = f32[3,1536,10]{1,2,0:T(8,128)S(1)} fusion(bf16[3,1536,10]{1,2,0:T(8,128)(2,1)S(1)} %reshape.268, f32[1536,1536]{1,0:T(8,128)} %bitcast_convert_fusion, f32[5,1536]{1,0:T(8,128)S(1)} %get-tuple-element.53, f32[5,1536]{1,0:T(8,128)S(1)} %get-tuple-element.54, bf16[5,1536]{1,0:T(8,128)(2,1)S(1)} %get-tuple-element.52, ...), kind=kOutput, calls=%fused_computation.5 | convolution fusion | flops 297378816 | bytes 9805824 | tf_op jit(solution)/shard_map/fap,kp->fak/dot_general | solution.py:132
  220.4 3.3 fusion.18
  223.8 13.8 %copy.205 = f32[3,2,4,5,1024]{2,1,4,3,0:T(2,128)} copy(f32[3,2,4,5,1024]{4,2,1,0,3:T(4,128)S(1)} %fusion.18) | data formatting | bytes 983040 | tf_op jit(solution)/shard_map/reshape | solution.py:140
  237.6 59.2 %gather_fusion.2 = f32[5120,3,2,4]{3,2,1,0:T(2,128)} fusion(f32[3,2,4,5120]{2,1,3,0:T(2,128)} %bitcast.116, s32[5120]{0:T(1024)S(1)} %broadcast_clamp_fusion), kind=kCustom, calls=%fused_computation.2 | custom fusion | bytes 1003520 | tf_op jit(solution)/shard_map/jit(_take)/gather | solution.py:139
  296.8 16.6 %copy.187 = f32[5120,3,2,4]{0,3,2,1:T(4,128)S(1)} copy(f32[5120,3,2,4]{3,2,1,0:T(2,128)} %gather_fusion.2) | data formatting | bytes 983040 | tf_op jit(solution)/shard_map/jit(_take)/gather | solution.py:139
  313.4 0.9 select_bitcast_fusion
  314.4 20.0 %all-reduce.2.cloned.1.call-done = f32[3,2,4,5120]{3,2,1,0:T(4,128)} async-done(((f32[3,2,4,5120]{3,2,1,0:T(4,128)}), f32[3,2,4,5120]{3,2,1,0:T(4,128)}) %all-reduce.2.cloned.1.call-update) | async-done | bytes 491536 | tf_op jit(solution)/shard_map/psum | solution.py:143
  334.5 1.3 constant_dynamic-slice_fusion.1
  335.7 3.6 collective-permute-start
  339.4 1.3 collective-permute-start.1
  340.7 1.0 constant_dynamic-slice_fusion.2
  341.6 0.7 collective-permute-done
  342.4 4.6 %collective-permute-done.1 = f32[3,2,2,2560]{3,2,1,0:T(2,128)S(1)} collective-permute-done((f32[3,2,2,2560]{3,2,1,0:T(2,128)S(1)}, f32[3,2,2,2560]{3,2,1,0:T(2,128)S(1)}, u32[]{:S(2)}, u32[]{:S(2)}) %collective-permute-start.1) | collective-permute-done | bytes 122912 | tf_op jit(solution)/shard_map/ppermute | solution.py:17
  346.9 0.5 fusion.33
  347.4 7.5 %copy.188 = f32[3,2,4,2560]{2,1,0,3:T(2,128)} copy(f32[3,2,4,2560]{3,2,1,0:T(4,128)S(1)} %fusion.33) | data formatting | bytes 491520 | tf_op jit(solution)/shard_map/add | solution.py:79
  354.9 11.5 %reshape.272 = f32[16,1,3840]{2,1,0:T(1,128)S(1)} reshape(f32[2560,3,2,4]{3,2,1,0:T(2,128)} %bitcast.114) | data formatting | bytes 491520
  366.4 15.6 %all_to_all.36 = f32[16,1,3840]{2,1,0:T(1,128)S(1)} all-to-all(f32[16,1,3840]{2,1,0:T(1,128)S(1)} %reshape.272), channel_id=1, replica_groups=mesh['rad'=16,'lat'=2] {'rad'}, dimensions={0} | all-to-all | bytes 491520 | tf_op jit(solution)/shard_map/all_to_all | solution.py:148
  382.1 0.5 broadcast.415
  382.6 1.2 reduce
  383.8 14.0 %reshape.273 = f32[2560,3,2,4]{3,2,1,0:T(2,128)} reshape(f32[16,3840]{1,0:T(8,128)S(1)} %reduce) | data formatting | bytes 491520
  397.8 9.8 %copy.206 = f32[3,2,4,16,160]{4,3,2,1,0:T(8,128)S(1)} copy(f32[3,2,4,16,160]{2,1,0,4,3:T(2,128)} %bitcast.115) | data formatting | bytes 491520 | tf_op jit(solution)/shard_map/all_to_all | solution.py:148
  407.6 0.3 copy.190
  407.9 0.8 copy.191
  (37 shorter events, 0.7 us)
Async XLA Ops:
  7.2 48.4 %copy-start = (s32[5120]{0:T(1024)S(1)}, s32[5120]{0:T(1024)}, u32[]{:S(2)}) copy-start(s32[5120]{0:T(1024)} %param.15) | copy-start | bytes 61444
  25.7 6.3 %copy-start.3 = (f32[160,32,32,1]{2,1,3,0:T(8,128)S(1)}, f32[160,32,32,1]{2,1,3,0:T(8,128)}, u32[]{:S(2)}) copy-start(f32[160,32,32,1]{2,1,3,0:T(8,128)} %copy.193) | copy-start | bytes 1966084
  25.7 6.3 %copy-start.4 = (f32[3,2,160,2,32]{4,0,1,2,3:T(4,128)S(1)}, f32[3,2,160,2,32]{4,0,1,2,3:T(4,128)}, u32[]{:S(2)}) copy-start(f32[3,2,160,2,32]{4,0,1,2,3:T(4,128)} %copy.170) | copy-start | bytes 737284
  32.0 8.5 %copy-start.2 = (f32[160,32,32,1]{2,1,3,0:T(8,128)S(1)}, f32[160,32,32,1]{2,1,3,0:T(8,128)}, u32[]{:S(2)}) copy-start(f32[160,32,32,1]{2,1,3,0:T(8,128)} %copy.195) | copy-start | bytes 1966084
  45.0 10.5 %copy-start.7 = (s32[5]{0:T(128)S(1)}, s32[5]{0:T(128)}, u32[]{:S(2)}) copy-start(s32[5]{0:T(128)} %param.14) | copy-start | bytes 64
  45.9 38.3 %copy-start.5 = (f32[3,2,160,2,32]{2,4,3,1,0:T(8,128)}, f32[3,2,160,2,32]{2,4,3,1,0:T(8,128)S(1)}, u32[]{:S(2)}) copy-start(f32[3,2,160,2,32]{2,4,3,1,0:T(8,128)S(1)} %copy.175) | copy-start | bytes 737284
  46.9 64.8 %all-to-all-start = ((bf16[3,2,64,160]{3,1,0,2:T(2,128)(2,1)}), bf16[3,2,64,160]{3,1,0,2:T(2,128)(2,1)S(1)}, u32[]{:S(2)}, u32[]{:S(2)}) async-start(bf16[3,2,64,160]{3,1,0,2:T(2,128)(2,1)} %copy.176), calls=%async_computation | async-start | bytes 393216 | tf_op jit(solution)/shard_map/all_to_all | solution.py:116
  55.2 279.3 %all-reduce.2.cloned.1.call-start = ((), (), s32[]{:S(2)}) async-start(), calls=%async_computation.2 | async-start | bytes 983040 | tf_op jit(solution)/shard_map/psum | solution.py:143
  209.2 11.2 %copy-start.6 = (f32[384]{0:T(512)S(1)}, f32[384]{0:T(512)}, u32[]{:S(2)}) copy-start(f32[384]{0:T(512)} %param.17) | copy-start | bytes 4612
  296.8 17.5 %copy-start.8 = (f32[64]{0:T(128)S(1)}, f32[64]{0:T(128)}, u32[]{:S(2)}) copy-start(f32[64]{0:T(128)} %param.19) | copy-start | bytes 772
  335.7 6.7 %collective-permute-start = (f32[3,2,2,2560]{3,2,1,0:T(2,128)S(1)}, f32[3,2,2,2560]{3,2,1,0:T(2,128)S(1)}, u32[]{:S(2)}, u32[]{:S(2)}) collective-permute-start(f32[3,2,2,2560]{3,2,1,0:T(2,128)S(1)} %get-tuple-element.49), channel_id=1, source_target_pairs={{0,2},{2,4},{4,6},{6,8},{8,10},{10,12},{12,14},{14,16},{16,18},{18... | collective-permute-start | bytes 368648 | tf_op jit(solution)/shard_map/ppermute | solution.py:16
  339.4 7.6 %collective-permute-start.1 = (f32[3,2,2,2560]{3,2,1,0:T(2,128)S(1)}, f32[3,2,2,2560]{3,2,1,0:T(2,128)S(1)}, u32[]{:S(2)}, u32[]{:S(2)}) collective-permute-start(f32[3,2,2,2560]{3,2,1,0:T(2,128)S(1)} %get-tuple-element.50), channel_id=1, source_target_pairs={{2,0},{4,2},{6,4},{8,6},{10,8},{12,10},{14,12},{16,14},{18,16},{20... | collective-permute-start | bytes 368648 | tf_op jit(solution)/shard_map/ppermute | solution.py:17
  397.8 10.9 %copy-start.1 = (s32[5120]{0:T(1024)S(1)}, s32[5120]{0:T(1024)}, u32[]{:S(2)}) copy-start(s32[5120]{0:T(1024)} %param.15) | copy-start | bytes 61444
Sparse Core Ops, SparseCore 0:
  314.4 19.9 all-reduce.1
where the time goes:
time: 420 us; the launch traced here: 416 us
  local copies, waits for them, and re-layouts  282 us (67%)
  matrix products  36.6 us (9%)
  blocking collectives  32.9 us (8%)
  waiting for transfers between devices  25.4 us (6%)
  between operations  14.6 us (3%)
  starting transfers between devices  13.3 us (3%)
  other arithmetic  11.4 us (3%)
    gather x2, local copies, waits for them, and re-layouts, body(): jnp.take(partial_value.reshape(item_count, 2, levels, slot_count), slot_a...  75.8 us
    gather x2, local copies, waits for them, and re-layouts, body(): jnp.take(gathered, pos_of_slot, axis=3)  70.2 us
    unnamed x23, local copies, waits for them, and re-layouts  32.1 us
    gather x1, local copies, waits for them, and re-layouts, body(): slot_at = jnp.take(slot_of_column, column)  28.7 us
    psum x1, waiting for transfers between devices, body(): summed = lax.psum(partial_value, 'lat')  20 us
    scatter x1, local copies, waits for them, and re-layouts, body(): pos_of_slot = jnp.zeros((slot_count,), jnp.int32).at[slot_at].set(positions)  19.3 us
    dot_general x4, matrix products, apply_block(): return jnp.einsum('kij,fckj->fcki', matrix, vector, precision=highest)  19.3 us
    all_gather x1, blocking collectives, body(): lax.all_gather(lax.all_to_all(level_major, 'rad', split_axis=2, concat_ax...  17.2 us
  transfers between devices with their start and end apart: 4, of which 3 were waited for; matrix products, arithmetic and copies ran while one was open for 14% of the time, Pallas kernels for 0%

commit v1 on v0

v1 whole, which is shorter than its diff:
```python
import functools
import math

import jax
import jax.numpy as jnp
from jax import lax
from jax.experimental import pallas as pl
from jax.experimental.pallas import tpu as pltpu
from jax.sharding import PartitionSpec as P

LANES = 128
LOW = 256
MESH = pl.DeviceIdType.MESH
VMEM = pl.BlockSpec(memory_space=pltpu.VMEM)
SMEM = pl.BlockSpec(memory_space=pltpu.SMEM)
F32 = jnp.float32
BF16 = jnp.bfloat16
ROOM = 48 * 1024 * 1024


def params(room=ROOM, **more):
    return pltpu.CompilerParams(vmem_limit_bytes=room, **more)


def phi_tables(slab_modes, phi_count, degree_count):
    columns = jnp.arange(phi_count, dtype=jnp.int32)
    residues = slab_modes[:, None] * columns[None, :] % phi_count
    angles = residues.astype(jnp.float32) * (2.0 * math.pi / phi_count)
    factor = slab_modes.astype(jnp.float32)[:, None] * (2.0 / degree_count)
    slope_table = jnp.concatenate([-factor * jnp.sin(angles), -factor * jnp.cos(angles)], 0).astype(
        jnp.bfloat16
    )
    back_table = (
        jnp.concatenate([jnp.cos(angles), -jnp.sin(angles)], 0) * (2.0 / phi_count)
    ).astype(jnp.bfloat16)
    return (slope_table, back_table)


class Blocks:
    def __init__(self, columns, values):
        self.columns, self.values = columns, values
        self.full, self.tail = divmod(columns, LANES)
        self.groups = values // 8
        self.packed = self.full > 0 and 0 < self.tail and self.tail * self.groups <= LANES
        self.packed = self.packed and LANES % self.tail == 0
        self.rows = self.full * values + 8 if self.packed else -(-columns // LANES) * values
        self.rows_held = -(-self.rows // 16) * 16
        self.share = LANES // self.tail if self.packed else 1

    def pack(self, value):
        parts = [value[:, i * LANES : (i + 1) * LANES] for i in range(self.full)]
        rest = value[:, self.full * LANES :]
        if self.packed:
            pieces = [rest[8 * g : 8 * g + 8] for g in range(self.groups)]
            spare = LANES - self.tail * self.groups
            if spare:
                pieces.append(jnp.zeros((8, spare), value.dtype))
            parts.append(jnp.concatenate(pieces, 1))
        elif self.tail:
            parts.append(
                jnp.concatenate([rest, jnp.zeros((self.values, LANES - self.tail), value.dtype)], 1)
            )
        if self.rows_held > self.rows:
            parts.append(jnp.zeros((self.rows_held - self.rows, LANES), value.dtype))
        return jnp.concatenate(parts, 0)

    def order(self, per_column, devices):
        table = per_column.reshape(devices, self.columns)
        whole = self.full if self.packed else -(-self.columns // LANES)
        if not self.packed and self.tail:
            table = jnp.pad(table, ((0, 0), (0, whole * LANES - self.columns)), constant_values=-1)
        parts = [table[:, : whole * LANES].reshape(-1)]
        if self.packed:
            parts.append(table[:, whole * LANES :].reshape(-1))
        return jnp.concatenate(parts)


def solve_kernel(blocks, ranks, forcing, pivots, lower, upper, solved, send, stage):
    items, depth, columns = forcing.shape
    count, size = pivots.shape[0], pivots.shape[1]
    levels = depth // ranks

    def apply_block(matrix, at, vectors):
        pieces = [[] for _ in vectors]
        for i in range(0, size, 8):
            rows = matrix[at, i : i + 8]
            for item, vector in enumerate(vectors):
                pieces[item].append(jnp.sum(rows * vector[None], axis=1))
        return [jnp.concatenate(p, 0) for p in pieces]

    def span(k):
        return pl.ds(k * size if isinstance(k, int) else pl.multiple_of(k * size, size), size)

    first = apply_block(pivots, 0, [forcing[item, span(0)] for item in range(items)])
    for item in range(items):
        solved[item, span(0)] = first[item]

    def descend(k, carry):
        drop = apply_block(lower, k - 1, carry)
        rest = [forcing[item, span(k)] - drop[item] for item in range(items)]
        now = apply_block(pivots, k, rest)
        for item in range(items):
            solved[item, span(k)] = now[item]
        return tuple(now)

    last = tuple(first)
    for k in range(1, count) if count <= 2 else ():
        last = descend(k, last)
    if count > 2:
        last = lax.fori_loop(1, count, descend, last)

    def up_step(step, carry):
        k = count - 2 - step
        drop = apply_block(upper, k, carry)
        now = [solved[item, span(k)] - drop[item] for item in range(items)]
        for item in range(items):
            solved[item, span(k)] = now[item]
        return tuple(now)

    if count <= 2:
        for step in range(count - 1):
            last = up_step(step, last)
    else:
        lax.fori_loop(0, count - 1, up_step, last)

    for rank in range(ranks):
        for item in range(items):
            stage[rank, item * levels : (item + 1) * levels, :] = solved[
                item, rank * levels : (rank + 1) * levels, :
            ]

    def give(rank, _):
        send[rank] = blocks.pack(stage[rank]).astype(BF16)
        return 0

    lax.fori_loop(0, ranks, give, 0)


def wave_kernel(modes, slope, back, zonal, out):
    levels = zonal.shape[0]
    parts = out.shape[0]
    s, b = slope[...].astype(F32), back[...].astype(F32)
    rows = []
    for e in range(2):
        for i in range(modes):
            for j in range(modes):
                for c in range(2):
                    a = c if e == 0 else 1 - c
                    rows.append(
                        s[a * modes + i : a * modes + i + 1] * b[c * modes + j : c * modes + j + 1]
                    )
    total = len(rows)
    spare = -total % 8
    table = jnp.concatenate(rows + [jnp.zeros((spare, s.shape[1]), F32)] * (spare > 0), 0)
    high = table.astype(BF16)
    low = (table - high.astype(F32)).astype(BF16)
    for r in range(levels):
        flow = zonal[r]
        dims = (((1,), (1,)), ((), ()))
        value = lax.dot_general(high, flow, dims, preferred_element_type=F32)
        value = value + lax.dot_general(low, flow, dims, preferred_element_type=F32)
        for part in range(parts):
            out[part, pl.ds(r, total, stride=levels), :] = value[
                :total, part * LANES : (part + 1) * LANES
            ]


def legendre_kernel(
    blocks, devices, ranks, modes_ref, slots, message, legendre, weight, waves, out,
    hot, spread, spectral, turned
):
    values = blocks.values
    modes, degrees, cycles = legendre.shape
    chunks = degrees // LOW
    total = slots.shape[1]
    whole = blocks.full if blocks.packed else -(-blocks.columns // LANES)
    main = devices * whole * LANES
    high_count = modes * chunks

    def side(at):
        return pl.ds(pl.multiple_of(at * LANES, LANES), LANES)

    def scatter(at, value):
        slot = slots[:, side(at)]
        high, low = slot // LOW, slot % LOW
        rows = lax.broadcasted_iota(jnp.int32, (LOW, LANES), 0)
        hot[:, side(at)] = jnp.where(rows == low, 1.0, 0.0).astype(BF16)
        for h in range(0, high_count, 2):
            pair = [jnp.where(high == h + n, value, 0.0) for n in range(2)]
            spread[h * values : (h + 2) * values, side(at)] = jnp.concatenate(pair, 0).astype(BF16)

    def main_step(device, _):
        block = message[device].astype(F32)
        for n in range(whole):
            scatter(device * whole + n, block[n * values : (n + 1) * values])
        return 0

    lax.fori_loop(0, devices, main_step, 0)

    if blocks.packed:
        share, tail = blocks.share, blocks.tail
        base = blocks.full * values

        def tail_step(group, _):
            held = [
                message[group * share + d].astype(F32)[base : base + 8] for d in range(share)
            ]
            pieces = [
                jnp.concatenate([h[:, g * tail : (g + 1) * tail] for h in held], 1)
                for g in range(blocks.groups)
            ]
            scatter(devices * whole + group, jnp.concatenate(pieces, 0))
            return 0

        lax.fori_loop(0, devices // share, tail_step, 0)

    coeffs = lax.dot_general(
        spread[...], hot[...], (((1,), (1,)), ((), ())), preferred_element_type=F32
    )
    lane = lax.broadcasted_iota(jnp.int32, (values, LOW), 1)

    def allowed(i, n):
        return lane + n * LOW >= modes_ref[i]

    for i in range(modes):
        rows = []
        for n in range(chunks):
            at = (i * chunks + n) * values
            rows.append(jnp.where(allowed(i, n), coeffs[at : at + values], 0.0).astype(BF16))
        value = jnp.dot(jnp.concatenate(rows, 1), legendre[i], preferred_element_type=F32)
        value = value.astype(BF16).astype(F32)
        spectral[i] = value
        for f in range(values // 8):
            block = value[f * 8 : f * 8 + 8]
            turned[i, f * 8 : f * 8 + 8] = jnp.concatenate([block[4:8], block[0:4]], 0)

    sums = []
    for j in range(modes):
        fields = []
        for f in range(values // 8):
            parts = []
            for part in range(cycles // LANES):
                acc = None
                for e, source in enumerate((spectral, turned)):
                    for i in range(modes):
                        at = ((e * modes + i) * modes + j) * 8
                        term = (
                            source[i, f * 8 : f * 8 + 8, part * LANES : (part + 1) * LANES]
                            * waves[part, at : at + 8, :]
                        )
                        acc = term if acc is None else acc + term
                parts.append(acc)
            fields.append(jnp.concatenate(parts, 1))
        sums.append((jnp.concatenate(fields, 0) * weight[...]).astype(BF16))

    pieces_high, pieces_low = [], []
    for i in range(modes):
        for n in range(chunks):
            value = lax.dot_general(
                sums[i], legendre[i, n * LOW : (n + 1) * LOW, :], (((1,), (1,)), ((), ())),
                preferred_element_type=F32,
            )
            value = jnp.where(allowed(i, n), value, 0.0)
            high = value.astype(BF16).astype(F32)
            pieces_high.append(high)
            pieces_low.append(value - high)
    both = jnp.concatenate(pieces_high + pieces_low, 0).astype(BF16)
    split = high_count * values

    def collect(at):
        value = jnp.dot(both, hot[:, side(at)], preferred_element_type=F32)
        high = slots[:, side(at)] // LOW
        acc = jnp.zeros((values, LANES), F32)
        for h in range(high_count):
            term = value[h * values : (h + 1) * values]
            term = term + value[split + h * values : split + (h + 1) * values]
            acc = acc + jnp.where(high == h, term, 0.0)
        return acc

    def back_step(device, _):
        for n in range(whole):
            out[device, n * values : (n + 1) * values, :] = collect(device * whole + n)
        return 0

    lax.fori_loop(0, devices, back_step, 0)

    if blocks.packed:

        def tail_back(group, _):
            value = collect(devices * whole + group)
            for d in range(share):
                pieces = [
                    value[g * 8 : g * 8 + 8, d * tail : (d + 1) * tail]
                    for g in range(blocks.groups)
                ]
                spare = LANES - tail * blocks.groups
                if spare:
                    pieces.append(jnp.zeros((8, spare), F32))
                out[group * share + d, base : base + 8, :] = jnp.concatenate(pieces, 1)
            return 0

        lax.fori_loop(0, devices // share, tail_back, 0)


def meet(ranks, me, other):
    barrier = pltpu.get_barrier_semaphore()

    def hello(d, _):
        pl.semaphore_signal(
            barrier, inc=1, device_id=(lax.rem(me + d, ranks), 1 - other), device_id_type=MESH
        )
        return 0

    def peers(d, _):
        pl.semaphore_signal(
            barrier, inc=1, device_id=(lax.rem(me + d, ranks), other), device_id_type=MESH
        )
        return 0

    hello(0, 0)
    lax.fori_loop(1, ranks, peers, 0)
    pl.semaphore_wait(barrier, ranks)


def forward_kernel(ranks, send, out, send_sem, recv_sem, pass_sem, got_sem, own_sem):
    me, lat = lax.axis_index("rad"), lax.axis_index("lat")
    meet(ranks, me, lat)

    def to_rank(rank, source):
        return pltpu.make_async_remote_copy(
            src_ref=send.at[rank],
            dst_ref=out.at[source, lat],
            send_sem=send_sem.at[rank],
            recv_sem=recv_sem.at[source],
            device_id=(rank, lat),
            device_id_type=MESH,
        )

    def to_pair(ref, source, half):
        return pltpu.make_async_remote_copy(
            src_ref=ref,
            dst_ref=out.at[source, half],
            send_sem=pass_sem.at[source],
            recv_sem=got_sem.at[source],
            device_id=(me, 1 - lat),
            device_id_type=MESH,
        )

    def begin(d, _):
        to_rank(lax.rem(me + d, ranks), me).start()
        return 0

    lax.fori_loop(1, ranks, begin, 0)
    to_pair(send.at[me], me, lat).start()
    own = pltpu.make_async_copy(send.at[me], out.at[me, lat], own_sem)
    own.start()

    def hand_on(d, _):
        source = lax.rem(me + ranks - d, ranks)
        to_rank(source, source).wait_recv()
        to_pair(out.at[source, lat], source, lat).start()
        return 0

    lax.fori_loop(1, ranks, hand_on, 0)
    own.wait()

    def finish(source, _):
        to_pair(out.at[source, lat], source, 1 - lat).wait()
        return 0

    lax.fori_loop(0, ranks, finish, 0)

    def sent(d, _):
        to_rank(lax.rem(me + d, ranks), me).wait_send()
        return 0

    lax.fori_loop(1, ranks, sent, 0)


def backward_kernel(
    ranks, partial, out, other, total, send_sem, recv_sem, pass_sem, got_sem
):
    me, lat = lax.axis_index("rad"), lax.axis_index("lat")
    meet(ranks, me, lat)

    def to_pair(rank):
        return pltpu.make_async_remote_copy(
            src_ref=partial.at[rank, 1 - lat],
            dst_ref=other.at[rank],
            send_sem=pass_sem.at[rank],
            recv_sem=got_sem.at[rank],
            device_id=(me, 1 - lat),
            device_id_type=MESH,
        )

    def to_rank(rank, source):
        return pltpu.make_async_remote_copy(
            src_ref=total.at[rank],
            dst_ref=out.at[source],
            send_sem=send_sem.at[rank],
            recv_sem=recv_sem.at[source],
            device_id=(rank, lat),
            device_id_type=MESH,
        )

    def begin(d, _):
        to_pair(lax.rem(me + d, ranks)).start()
        return 0

    lax.fori_loop(1, ranks + 1, begin, 0)

    def add(d, _):
        rank = lax.rem(me + d, ranks)
        to_pair(rank).wait_recv()
        total[rank] = (partial[rank, lat] + other[rank]).astype(total.dtype)
        to_rank(rank, me).start()
        return 0

    lax.fori_loop(1, ranks, add, 0)
    to_pair(me).wait_recv()
    out[me] = (partial[me, lat] + other[me]).astype(out.dtype)

    def finish(d, _):
        source = lax.rem(me + ranks - d, ranks)
        to_rank(source, source).wait_recv()
        return 0

    lax.fori_loop(1, ranks, finish, 0)

    def sent(d, _):
        to_rank(lax.rem(me + d, ranks), me).wait_send()
        return 0

    lax.fori_loop(1, ranks, sent, 0)

    def passed(rank, _):
        to_pair(rank).wait_send()
        return 0

    lax.fori_loop(0, ranks, passed, 0)


def stencil_kernel(blocks, ranks, spacing, got, out, held):
    items, depth, columns = out.shape
    levels = depth // ranks
    values = blocks.values
    edge = 8
    held[:, 0:edge, :] = jnp.zeros((items, edge, columns), F32)
    held[:, edge + depth : 2 * edge + depth, :] = jnp.zeros((items, edge, columns), F32)

    for rank in range(ranks):
        value = got[rank].astype(F32)
        parts = [value[n * values : (n + 1) * values] for n in range(blocks.full)]
        if blocks.packed:
            base = blocks.full * values
            parts.append(
                jnp.concatenate(
                    [
                        value[base : base + 8, g * blocks.tail : (g + 1) * blocks.tail]
                        for g in range(blocks.groups)
                    ],
                    0,
                )
            )
        elif blocks.tail:
            base = blocks.full * values
            parts.append(value[base : base + values, : blocks.tail])
        at = edge + rank * levels
        lane = 0
        for part in parts:
            width = part.shape[1]
            for item in range(items):
                held[item, at : at + levels, lane : lane + width] = part[
                    item * levels : (item + 1) * levels
                ]
            lane += width

    factor = spacing[...]
    for item in range(items):
        def shifted(n):
            return held[item, edge + n : edge + n + depth, :]

        slope = shifted(-2) - 8.0 * shifted(-1) + 8.0 * shifted(1) - shifted(2)
        out[item] = shifted(0) + factor * slope


def body(
    forcing,
    pivots,
    lower,
    upper,
    slab_modes,
    slot_of_column,
    legendre,
    cycle_weight,
    zonal_flow,
    inverse_spacing,
):
    ranks, halves = lax.axis_size("rad"), lax.axis_size("lat")
    devices = ranks * halves
    columns, depth = forcing.shape[2], forcing.shape[3]
    modes, degrees, cycles = legendre.shape
    levels, _, phi_count = zonal_flow.shape
    items = 6
    values = items * levels
    blocks = Blocks(columns, values)
    rows = blocks.rows_held

    right = forcing.transpose(0, 1, 3, 2).reshape(items, depth, columns)
    solved, send = pl.pallas_call(
        functools.partial(solve_kernel, blocks, ranks),
        out_shape=(
            jax.ShapeDtypeStruct((items, depth, columns), F32),
            jax.ShapeDtypeStruct((ranks, rows, LANES), BF16),
        ),
        in_specs=[VMEM] * 4,
        out_specs=(VMEM, VMEM),
        scratch_shapes=[pltpu.VMEM((ranks, values, columns), F32)],
        compiler_params=params(),
        name="solve",
    )(right, *(m.transpose(1, 2, 3, 0) for m in (pivots, lower, upper)))

    got = pl.pallas_call(
        functools.partial(forward_kernel, ranks),
        out_shape=jax.ShapeDtypeStruct((ranks, halves, rows, LANES), BF16),
        in_specs=[VMEM],
        out_specs=VMEM,
        scratch_shapes=[pltpu.SemaphoreType.DMA((ranks,))] * 4 + [pltpu.SemaphoreType.DMA],
        compiler_params=params(collective_id=0, has_side_effects=True),
        name="forward",
    )(send)

    slope_table, back_table = phi_tables(slab_modes, phi_count, degrees)
    waves = pl.pallas_call(
        functools.partial(wave_kernel, modes),
        out_shape=jax.ShapeDtypeStruct(
            (cycles // LANES, 4 * modes * modes * levels, LANES), F32
        ),
        in_specs=[VMEM] * 3,
        out_specs=VMEM,
        compiler_params=params(),
        name="waves",
    )(slope_table, back_table, zonal_flow)

    slots = blocks.order(slot_of_column, devices)[None]
    total = slots.shape[1]
    high_count = modes * (degrees // LOW)
    partial = pl.pallas_call(
        functools.partial(legendre_kernel, blocks, devices, ranks),
        out_shape=jax.ShapeDtypeStruct((devices, rows, LANES), F32),
        in_specs=[SMEM] + [VMEM] * 5,
        out_specs=VMEM,
        scratch_shapes=[
            pltpu.VMEM((LOW, total), BF16),
            pltpu.VMEM((high_count * values, total), BF16),
            pltpu.VMEM((modes, values, cycles), F32),
            pltpu.VMEM((modes, values, cycles), F32),
        ],
        compiler_params=params(ROOM if total <= 8192 else 60 * 1024 * 1024),
        name="legendre",
    )(slab_modes, slots, got.reshape(devices, rows, LANES), legendre, cycle_weight[None], waves)

    back = pl.pallas_call(
        functools.partial(backward_kernel, ranks),
        out_shape=jax.ShapeDtypeStruct((ranks, rows, LANES), F32),
        in_specs=[VMEM],
        out_specs=VMEM,
        scratch_shapes=[
            pltpu.VMEM((ranks, rows, LANES), F32),
            pltpu.VMEM((ranks, rows, LANES), F32),
        ]
        + [pltpu.SemaphoreType.DMA((ranks,))] * 4,
        compiler_params=params(collective_id=1, has_side_effects=True),
        name="backward",
    )(partial.reshape(ranks, halves, rows, LANES))

    explicit = pl.pallas_call(
        functools.partial(stencil_kernel, blocks, ranks),
        out_shape=jax.ShapeDtypeStruct((items, depth, columns), F32),
        in_specs=[VMEM] * 2,
        out_specs=VMEM,
        scratch_shapes=[pltpu.VMEM((items, depth + 16, columns), F32)],
        compiler_params=params(),
        name="stencil",
    )(inverse_spacing[:, None], back)

    def placed(value):
        return value.reshape(3, 2, depth, columns).transpose(0, 1, 3, 2)

    return (placed(solved), placed(explicit))


def solution(mesh):
    placed = (
        P(None, None, ("rad", "lat"), None),
        P(("rad", "lat"), None, None, None),
        P(("rad", "lat"), None, None, None),
        P(("rad", "lat"), None, None, None),
        P(),
        P(),
        P(None, None, "lat"),
        P("lat"),
        P("rad", "lat", None),
        P(),
    )
    return jax.shard_map(
        body,
        mesh=mesh,
        in_specs=placed,
        out_specs=(P(None, None, ("rad", "lat"), None), P(None, None, ("rad", "lat"), None)),
        check_vma=False,
    )
```

time: 420 us -> 63 us (0.15)
  local copies, waits for them, and re-layouts: 282 us -> 5.3 us
  Pallas kernels: 0 us -> 55 us
  matrix products: 36.6 us -> 0 us
  blocking collectives: 32.9 us -> 0 us
  waiting for transfers between devices: 25.4 us -> 0 us
  between operations: 14.6 us -> 0.79 us
  starting transfers between devices: 13.3 us -> 0 us
  other arithmetic: 11.4 us -> 1.71 us
    gather x5 -> x0, local copies, waits for them, and re-layouts: 175 us -> none  [the longest x2 75.8 us: body(): jnp.take(partial_value.reshape(item_count, 2, levels, slot_count), slot_a...]
    pallas_call x0 -> x6, Pallas kernels: none -> 55 us  [the longest x1 21.4 us: body(): pl.pallas_call(functools.partial(legendre_kernel, blocks, devices, ranks)...]
    dot_general x7 -> x0, matrix products: 36.6 us -> none  [the longest x4 19.3 us: apply_block(): return jnp.einsum('kij,fckj->fcki', matrix, vector, precision=highest)]
    unnamed x23 -> x20, local copies, waits for them, and re-layouts: 32.1 us -> 5.05 us
    psum x1 -> x0, waiting for transfers between devices: 20 us -> none  [body(): summed = lax.psum(partial_value, 'lat')]
    scatter x1 -> x0, local copies, waits for them, and re-layouts: 19.3 us -> none  [body(): pos_of_slot = jnp.zeros((slot_count,), jnp.int32).at[slot_at].set(positions)]
    all_to_all x5 -> x0, local copies, waits for them, and re-layouts: 17.6 us -> none  [the longest x3 10.6 us: body(): lax.all_to_all(explicit_part, 'rad', split_axis=3, concat_axis=2, tiled=T...]
    all_gather x1 -> x0, blocking collectives: 17.2 us -> none  [body(): lax.all_gather(lax.all_to_all(level_major, 'rad', split_axis=2, concat_ax...]
  transfers between devices with their start and end apart: 4 -> 0, of which waited for: 3 -> 0; matrix products, arithmetic and copies ran while one was open for 14% -> 0% of each run, Pallas kernels for 0% -> 0%
where the time goes in v1:
time: 63 us; the launch traced here: 62.8 us
  Pallas kernels  55 us (87%)
  local copies, waits for them, and re-layouts  5.3 us (8%)
  other arithmetic  1.71 us (3%)
  between operations  0.79 us (1%)
    pallas_call x1, Pallas kernels, body(): pl.pallas_call(functools.partial(legendre_kernel, blocks, devices, ranks)...  21.4 us
    pallas_call x1, Pallas kernels, body(): pl.pallas_call(functools.partial(backward_kernel, ranks), out_shape=jax.S...  12.2 us
    pallas_call x1, Pallas kernels, body(): pl.pallas_call(functools.partial(forward_kernel, ranks), out_shape=jax.Sh...  11.7 us
    pallas_call x1, Pallas kernels, body(): pl.pallas_call(functools.partial(solve_kernel, blocks, ranks), out_shape=...  5.57 us
    unnamed x20, local copies, waits for them, and re-layouts  5.05 us
    pallas_call x1, Pallas kernels, body(): pl.pallas_call(functools.partial(wave_kernel, modes), out_shape=jax.Shape...  3.04 us

profile of v1, /device:TPU:0, one launch (start us, length us, event | category | flops | bytes accessed | tf_op | source)
XLA Modules:
  0.0 62.8 jit_solution(12201804248408870992)
XLA Ops:
  0.6 0.0 copy-start.5
  0.6 0.7 %multiply_negate_fusion = f32[5]{0:T(128)S(1)} fusion(s32[5]{0:T(128)} %modes_ref.1), kind=kLoop, calls=%fused_computation.17 | loop fusion | flops 15 | bytes 40 | tf_op jit(solution)/shard_map/neg | solution.py:30
  1.3 0.9 %fusion.5 = (f32[5,1536]{1,0:T(8,128)S(1)}, f32[5,1536]{1,0:T(8,128)S(1)}, bf16[5,1536]{1,0:T(8,128)(2,1)S(1)}, bf16[5,1536]{1,0:T(8,128)(2,1)S(1)}) fusion(s32[5]{0:T(128)} %modes_ref.1, f32[5]{0:T(128)S(1)} %multiply_negate_fusion), kind=kLoop, calls=%fused_computation.11 | loop fusion | flops 107520 | bytes 92200 | tf_op jit(solution)/shard_map/cos | solution.py:30
  2.4 0.0 copy-start
  2.4 2.3 %copy-done = bf16[4,384,1536]{2,1,0:T(8,128)(2,1)S(1)} copy-done((bf16[4,384,1536]{2,1,0:T(8,128)(2,1)S(1)}, bf16[4,384,1536]{2,1,0:T(8,128)(2,1)}, u32[]{:S(2)}) %copy-start) | copy-done | bytes 4718616
  4.7 0.0 copy-start.7
  4.7 0.0 copy-start.2
  4.7 3.0 %waves.1 = f32[3,400,128]{2,1,0:T(8,128)S(1)} custom-call(bf16[10,1536]{1,0:T(8,128)(2,1)S(1)} %pad_maximum_fusion.slope, bf16[10,1536]{1,0:T(8,128)(2,1)S(1)} %fusion.back, bf16[4,384,1536]{2,1,0:T(8,128)(2,1)S(1)} %copy-done), custom_call_target="tpu_custom_call" | custom-call | tf_op jit(solution)/shard_map/waves/pallas_call | solution.py:534
  7.7 0.0 copy-done.7
  7.8 0.0 copy-start.8
  7.8 0.0 copy-start.6
  7.8 0.1 reshape.34
  7.9 0.1 reshape.36
  7.9 0.0 copy-start.1
  7.9 0.0 copy-done.5
  8.0 0.0 copy-done.2
  8.0 0.0 copy-start.3
  8.0 1.4 %copy-done.3 = f32[160,1,32,32]{0,3,2,1:T(8,128)S(1)} copy-done((f32[160,1,32,32]{0,3,2,1:T(8,128)S(1)}, f32[160,1,32,32]{0,3,2,1:T(8,128)}, u32[]{:S(2)}) %copy-start.3) | copy-done | bytes 655384
  9.3 0.0 copy-start.4
  9.3 1.3 %copy-done.4 = f32[160,1,32,32]{0,3,2,1:T(8,128)S(1)} copy-done((f32[160,1,32,32]{0,3,2,1:T(8,128)S(1)}, f32[160,1,32,32]{0,3,2,1:T(8,128)}, u32[]{:S(2)}) %copy-start.4) | copy-done | bytes 655384
  10.7 5.6 %solve.1 = (f32[6,64,160]{2,1,0:T(8,128)}, bf16[16,32,128]{2,1,0:T(8,128)(2,1)S(1)}) custom-call(f32[6,64,160]{2,1,0:T(8,128)S(1)} %bitcast.23, f32[2,32,32,160]{3,2,1,0:T(8,128)S(1)} %bitcast.18, f32[1,32,32,160]{3,2,1,0:T(8,128)S(1)} %bitcast.21, f32[1,32,32,160]{3,2,1,0:T(8,128)S(1)} %bitcast.22), custom_call_target="tpu_custom_call" | custom-call | tf_op jit(solution)/shard_map/solve/pallas_call | solution.py:510
  16.2 0.0 copy-start.9
  16.2 11.7 %forward.1 = bf16[16,2,32,128]{3,2,1,0:T(8,128)(2,1)S(1)} custom-call(bf16[16,32,128]{2,1,0:T(8,128)(2,1)S(1)} %get-tuple-element.5.send), custom_call_target="tpu_custom_call" | custom-call | tf_op jit(solution)/shard_map/forward/pallas_call | solution.py:523
  27.9 0.0 copy-done.8
  27.9 0.0 copy-done.6
  27.9 0.0 copy-done.1
  27.9 21.4 %legendre.2 = f32[32,32,128]{2,1,0:T(8,128)S(1)} custom-call(s32[5]{0:T(128)S(1)} %copy-done.6, s32[1,5120]{1,0:T(1,128)S(1)} %bitcast.24, bf16[32,32,128]{2,1,0:T(8,128)(2,1)S(1)} %bitcast.20, bf16[5,1024,384]{2,1,0:T(8,128)(2,1)S(1)} %copy-done.1, f32[1,384]{1,0:T(1,128)S(1)} %broadcast_in_dim.14.weight, f32[3,400,128]{2,1,0:T(8,128)S(1)} %waves.1), custom_call_target="tpu_custom_call" | custom-call | tf_op jit(solution)/shard_map/legendre/pallas_call | solution.py:548
  49.4 12.2 %backward.1.got = f32[16,32,128]{2,1,0:T(8,128)S(1)} custom-call(f32[16,2,32,128]{3,2,1,0:T(8,128)S(1)} %bitcast.19), custom_call_target="tpu_custom_call" | custom-call | tf_op jit(solution)/shard_map/backward/pallas_call | solution.py:563
  61.6 0.0 copy-done.9
  61.6 0.1 copy.12.spacing
  61.7 1.0 %stencil.1 = f32[6,64,160]{2,1,0:T(8,128)} custom-call(f32[64,1]{1,0:T(8,128)S(1)} %copy.12.spacing, f32[16,32,128]{2,1,0:T(8,128)S(1)} %backward.1.got), custom_call_target="tpu_custom_call" | custom-call | tf_op jit(solution)/shard_map/stencil/pallas_call | solution.py:577
  (6 shorter events, 0.1 us)
Async XLA Ops:
  0.6 7.3 %copy-start.5 = (f32[3,2,160,64]{2,3,1,0:T(8,128)S(1)}, f32[3,2,160,64]{2,3,1,0:T(8,128)}, u32[]{:S(2)}) copy-start(f32[3,2,160,64]{2,3,1,0:T(8,128)} %param.10) | copy-start | bytes 737284
  2.4 2.3 %copy-start = (bf16[4,384,1536]{2,1,0:T(8,128)(2,1)S(1)}, bf16[4,384,1536]{2,1,0:T(8,128)(2,1)}, u32[]{:S(2)}) copy-start(bf16[4,384,1536]{2,1,0:T(8,128)(2,1)} %zonal.1) | copy-start | bytes 14155780
  4.7 3.1 %copy-start.7 = (s32[5120]{0:T(1024)S(1)}, s32[5120]{0:T(1024)}, u32[]{:S(2)}) copy-start(s32[5120]{0:T(1024)} %param.15) | copy-start | bytes 61444
  4.7 3.3 %copy-start.2 = (f32[160,2,32,32]{0,3,2,1:T(8,128)S(1)}, f32[160,2,32,32]{0,3,2,1:T(8,128)}, u32[]{:S(2)}) copy-start(f32[160,2,32,32]{0,3,2,1:T(8,128)} %param.11) | copy-start | bytes 3932164
  7.8 20.1 %copy-start.8 = (f32[384]{0:T(512)S(1)}, f32[384]{0:T(512)}, u32[]{:S(2)}) copy-start(f32[384]{0:T(512)} %param.17) | copy-start | bytes 4612
  7.8 20.2 %copy-start.6 = (s32[5]{0:T(128)S(1)}, s32[5]{0:T(128)}, u32[]{:S(2)}) copy-start(s32[5]{0:T(128)} %modes_ref.1) | copy-start | bytes 64
  7.9 20.0 %copy-start.1 = (bf16[5,1024,384]{2,1,0:T(8,128)(2,1)S(1)}, bf16[5,1024,384]{2,1,0:T(8,128)(2,1)}, u32[]{:S(2)}) copy-start(bf16[5,1024,384]{2,1,0:T(8,128)(2,1)} %legendre.3) | copy-start | bytes 11796484
  8.0 1.4 %copy-start.3 = (f32[160,1,32,32]{0,3,2,1:T(8,128)S(1)}, f32[160,1,32,32]{0,3,2,1:T(8,128)}, u32[]{:S(2)}) copy-start(f32[160,1,32,32]{0,3,2,1:T(8,128)} %param.12) | copy-start | bytes 1966084
  9.3 1.3 %copy-start.4 = (f32[160,1,32,32]{0,3,2,1:T(8,128)S(1)}, f32[160,1,32,32]{0,3,2,1:T(8,128)}, u32[]{:S(2)}) copy-start(f32[160,1,32,32]{0,3,2,1:T(8,128)} %param.13) | copy-start | bytes 1966084
  16.2 45.4 %copy-start.9 = (f32[64]{0:T(128)S(1)}, f32[64]{0:T(128)}, u32[]{:S(2)}) copy-start(f32[64]{0:T(128)} %param.19) | copy-start | bytes 772

commit v2 on v0

v2 whole, which is shorter than its diff:
```python
import functools
import math

import jax
import jax.numpy as jnp
from jax import lax
from jax.experimental import pallas as pl
from jax.experimental.pallas import tpu as pltpu
from jax.sharding import PartitionSpec as P

LANES = 128
SHIFT = 8
LOW = 1 << SHIFT
MESH = pl.DeviceIdType.MESH
VMEM = pl.BlockSpec(memory_space=pltpu.VMEM)
SMEM = pl.BlockSpec(memory_space=pltpu.SMEM)
ANY = pl.BlockSpec(memory_space=pl.ANY)
F32 = jnp.float32
BF16 = jnp.bfloat16
ROOM = 60 * 1024 * 1024


class Blocks:
    def __init__(self, columns, values, ranks):
        self.columns, self.values, self.ranks = columns, values, ranks
        self.full, self.tail = divmod(columns, LANES)
        self.groups = values // 8
        self.slot = 8
        while self.slot < self.tail:
            self.slot *= 2
        assert self.full <= 1 and self.slot * self.groups <= LANES
        self.base = self.full * values
        self.rows = -(-(self.base + 8) // 16) * 16
        self.share = LANES // self.slot
        self.main = ranks * self.full * LANES
        self.half = self.main + ranks * self.slot

    def join(self, main, tail):
        parts = ([main] if self.full else []) + [tail]
        spare = self.rows - self.base - 8
        if spare:
            parts.append(jnp.zeros((spare, LANES), tail.dtype))
        return jnp.concatenate(parts, 0)

    def lanes(self, pieces):
        parts = []
        for piece in pieces:
            parts.append(piece)
            if piece.shape[1] < self.slot:
                parts.append(jnp.zeros((8, self.slot - piece.shape[1]), piece.dtype))
        spare = LANES - self.slot * len(pieces)
        if spare:
            parts.append(jnp.zeros((8, spare), pieces[0].dtype))
        return jnp.concatenate(parts, 1)

    def pack(self, value):
        rest = value[:, self.full * LANES :]
        tail = self.lanes([rest[8 * g : 8 * g + 8] for g in range(self.groups)])
        return self.join(value[:, : self.full * LANES], tail)

    def order(self, per_column, halves):
        table = per_column.reshape(self.ranks, halves, self.columns).transpose(1, 0, 2)
        main = table[:, :, : self.full * LANES].reshape(halves, self.main)
        tail = table[:, :, self.full * LANES :]
        tail = jnp.pad(
            tail, ((0, 0), (0, 0), (0, self.slot - self.tail)), constant_values=-1
        ).reshape(halves, self.ranks * self.slot)
        return jnp.concatenate([main, tail], 1).reshape(1, halves * self.half)


def sublane_sums(values):
    row = lax.broadcasted_iota(jnp.int32, values[0].shape, 0)
    step = 1
    while len(values) > 1:
        keep = (row & step) == 0
        merged = []
        for first, second in zip(values[0::2], values[1::2]):
            straight = jnp.where(keep, first, second)
            crossed = jnp.where(keep, second, first)
            merged.append(straight + pltpu.roll(crossed, step, 0))
        values, step = merged, step * 2
    return values[0]


def kernel(
    blocks, halves, modes_ref, slots, spacing, weight, forcing_hbm, pivots_hbm, lower_hbm,
    upper_hbm, zonal_hbm, legendre_hbm, solved_hbm, out,
    forcing, pivots, lower, upper, zonal, legendre, solved, stage, send, message, hot, spread,
    waves, spectral, turned, tails, give, other, total, back, held,
    load_sem, solved_sem, send_sem, recv_sem, pass_sem, got_sem,
    send2_sem, recv2_sem, pass2_sem, got2_sem,
):
    me, lat = lax.axis_index("rad"), lax.axis_index("lat")
    ranks, values, base = blocks.ranks, blocks.values, blocks.base
    items, depth, columns = forcing.shape
    count, size = pivots.shape[0], pivots.shape[1]
    levels = depth // ranks
    modes, degrees, cycles = legendre.shape
    phi_count = zonal.shape[2]
    chunks = degrees // LOW
    high_count = modes * chunks
    fields = values // 8

    loads = [
        pltpu.make_async_copy(source, target, load_sem.at[n])
        for n, (source, target) in enumerate(
            (
                (forcing_hbm, forcing), (pivots_hbm, pivots), (lower_hbm, lower),
                (upper_hbm, upper), (zonal_hbm, zonal), (legendre_hbm, legendre),
            )
        )
    ]
    for load in loads:
        load.start()

    barrier = pltpu.get_barrier_semaphore()
    pl.semaphore_signal(barrier, inc=1, device_id=(me, 1 - lat), device_id_type=MESH)

    def hello(d, _):
        rank = lax.rem(me + d, ranks)
        pl.semaphore_signal(barrier, inc=1, device_id=(rank, lat), device_id_type=MESH)
        return 0

    lax.fori_loop(1, ranks, hello, 0)

    def to_rank(rank, source):
        return pltpu.make_async_remote_copy(
            src_ref=send.at[rank], dst_ref=message.at[lat, source],
            send_sem=send_sem.at[rank], recv_sem=recv_sem.at[source],
            device_id=(rank, lat), device_id_type=MESH,
        )

    def to_pair(source, half):
        return pltpu.make_async_remote_copy(
            src_ref=message.at[lat, source], dst_ref=message.at[half, source],
            send_sem=pass_sem.at[source], recv_sem=got_sem.at[source],
            device_id=(me, 1 - lat), device_id_type=MESH,
        )

    def apply_block(matrix, at, vectors):
        pieces = [[] for _ in vectors]
        for i in range(0, size, 8):
            for item, vector in enumerate(vectors):
                sums = []
                for n in range(8):
                    acc = matrix[at, i + n, 0:8] * vector[0:8]
                    for j in range(8, size, 8):
                        acc = acc + matrix[at, i + n, j : j + 8] * vector[j : j + 8]
                    sums.append(acc)
                pieces[item].append(sublane_sums(sums))
        return [jnp.concatenate(p, 0) for p in pieces]

    def span(k):
        return pl.ds(k * size if isinstance(k, int) else pl.multiple_of(k * size, size), size)

    per_block = size // levels

    def emit(k, vectors):
        for u in range(per_block):
            for item in range(items):
                stage[k * per_block + u, item * levels : (item + 1) * levels, :] = vectors[item][
                    u * levels : (u + 1) * levels
                ]

        def give_one(u, _):
            rank = k * per_block + u
            send[rank] = blocks.pack(stage[rank]).astype(BF16)

            @pl.when(rank != me)
            def _():
                to_rank(rank, me).start()

            return 0

        lax.fori_loop(0, per_block, give_one, 0)

    loads[0].wait()
    loads[1].wait()
    first = apply_block(pivots, 0, [forcing[item, span(0)] for item in range(items)])
    for item in range(items):
        solved[item, span(0)] = first[item]
    loads[2].wait()

    def descend(k, carry):
        drop = apply_block(lower, k - 1, carry)
        rest = [forcing[item, span(k)] - drop[item] for item in range(items)]
        now = apply_block(pivots, k, rest)
        for item in range(items):
            solved[item, span(k)] = now[item]
        return tuple(now)

    last = tuple(first)
    if count == 2:
        last = descend(1, last)
    else:
        last = lax.fori_loop(1, count, descend, last)
    loads[3].wait()
    pl.semaphore_wait(barrier, ranks)
    emit(count - 1, last)

    def up_step(step, carry):
        k = count - 2 - step
        drop = apply_block(upper, k, carry)
        now = [solved[item, span(k)] - drop[item] for item in range(items)]
        for item in range(items):
            solved[item, span(k)] = now[item]
        emit(k, now)
        return tuple(now)

    if count == 2:
        up_step(0, last)
    else:
        lax.fori_loop(0, count - 1, up_step, last)
    keep = pltpu.make_async_copy(solved, solved_hbm, solved_sem)
    keep.start()
    message[lat, me] = send[me]
    to_pair(me, lat).start()

    loads[4].wait()
    row = lax.broadcasted_iota(jnp.int32, (8, phi_count), 0)
    column = lax.broadcasted_iota(jnp.int32, (8, phi_count), 1).astype(F32)
    wave = jnp.zeros((8, phi_count), F32)
    for i in range(modes):
        wave = jnp.where(row == i, modes_ref[i].astype(F32), wave)
    turns = wave * column
    turns = turns - phi_count * jnp.floor((turns + 0.5) * (1.0 / phi_count))
    angle = turns * (2.0 * math.pi / phi_count)
    sine, cosine = jnp.sin(angle), jnp.cos(angle)
    factor = wave * (2.0 / degrees)
    slope = [(-factor * t).astype(BF16).astype(F32) for t in (sine, cosine)]
    turn = [(t * (2.0 / phi_count)).astype(BF16).astype(F32) for t in (cosine, -sine)]
    rows = []
    for c in range(2):
        for e in range(2):
            for i in range(modes):
                rows.append(slope[c if e == 0 else 1 - c][i : i + 1] * turn[c])
    table = jnp.concatenate(rows, 0)
    high = table.astype(BF16)
    rest = (table - high.astype(F32)).astype(BF16)
    tables = jnp.concatenate([high, rest], 0)
    across = (((1,), (1,)), ((), ()))
    pairs = 2 * modes * 8
    for r in range(levels):
        value = lax.dot_general(tables, zonal[r], across, preferred_element_type=F32)
        value = value[: 2 * pairs] + value[2 * pairs :]
        for c in range(2):
            for part in range(cycles // LANES):
                waves[part, pl.ds(c * levels + r, pairs, stride=8), :] = value[
                    c * pairs : (c + 1) * pairs, part * LANES : (part + 1) * LANES
                ]

    def lay(at, value):
        here = pl.ds(pl.multiple_of(at, LANES), LANES)
        high = lax.shift_right_arithmetic(slots[:, here], SHIFT)
        for h in range(0, high_count, 2):
            pair = [jnp.where(high == h + n, value, 0.0) for n in range(2)]
            spread[h * values : (h + 2) * values, here] = jnp.concatenate(pair, 0).astype(BF16)

    def lay_main(half, source):
        if blocks.full:
            lay(half * blocks.half + source * LANES, message[half, source].astype(F32)[:values])

    def lay_tails(half):
        share, slot = blocks.share, blocks.slot

        def step(group, _):
            sets = [
                message[half, group * share + d].astype(F32)[base : base + 8]
                for d in range(share)
            ]
            pieces = [
                jnp.concatenate([s[:, g * slot : (g + 1) * slot] for s in sets], 1)
                for g in range(blocks.groups)
            ]
            at = half * blocks.half + blocks.main + group * LANES
            lay(at, jnp.concatenate(pieces, 0))
            return 0

        lax.fori_loop(0, ranks // share, step, 0)

    def hand_on(d, _):
        source = lax.rem(me + ranks - d, ranks)
        to_rank(source, source).wait_recv()
        to_pair(source, lat).start()
        return 0

    lax.fori_loop(1, ranks, hand_on, 0)

    def heat(n, _):
        here = pl.ds(pl.multiple_of(n * LANES, LANES), LANES)
        low = slots[:, here] & (LOW - 1)
        rows = lax.broadcasted_iota(jnp.int32, (LOW, LANES), 0)
        hot[:, here] = jnp.where(rows == low, 1.0, 0.0).astype(BF16)
        return 0

    lax.fori_loop(0, halves * blocks.half // LANES, heat, 0)

    def mine(source, _):
        lay_main(lat, source)
        return 0

    lax.fori_loop(0, ranks, mine, 0)
    lay_tails(lat)

    def theirs(source, _):
        to_pair(source, 1 - lat).wait_recv()
        lay_main(1 - lat, source)
        return 0

    lax.fori_loop(0, ranks, theirs, 0)
    lay_tails(1 - lat)

    coeffs = lax.dot_general(spread[...], hot[...], across, preferred_element_type=F32)
    lane = lax.broadcasted_iota(jnp.int32, (values, LOW), 1)

    def allowed(i, n):
        return lane + n * LOW >= modes_ref[i]

    loads[5].wait()
    for i in range(modes):
        rows = []
        for n in range(chunks):
            at = (i * chunks + n) * values
            rows.append(jnp.where(allowed(i, n), coeffs[at : at + values], 0.0).astype(BF16))
        value = jnp.dot(jnp.concatenate(rows, 1), legendre[i], preferred_element_type=F32)
        value = value.astype(BF16).astype(F32)
        spectral[i] = value
        for f in range(fields):
            turned[i, f * 8 : f * 8 + 8] = pltpu.roll(value[f * 8 : f * 8 + 8], 4, 0)

    sums = []
    for j in range(modes):
        stack = []
        for f in range(fields):
            parts = []
            for part in range(cycles // LANES):
                acc = None
                for e, source in enumerate((spectral, turned)):
                    for i in range(modes):
                        at = ((e * modes + i) * 8 + j) * 8
                        term = (
                            source[i, f * 8 : f * 8 + 8, part * LANES : (part + 1) * LANES]
                            * waves[part, at : at + 8, :]
                        )
                        acc = term if acc is None else acc + term
                parts.append(acc)
            stack.append(jnp.concatenate(parts, 1))
        sums.append((jnp.concatenate(stack, 0) * weight[...]).astype(BF16))

    pieces = []
    for i in range(modes):
        value = lax.dot_general(sums[i], legendre[i], across, preferred_element_type=F32)
        for n in range(chunks):
            piece = value[:, n * LOW : (n + 1) * LOW]
            pieces.append(jnp.where(allowed(i, n), piece, 0.0))
    advection = jnp.concatenate(pieces, 0).astype(BF16)

    wide = 2 * LANES

    def collect(at):
        here = pl.ds(pl.multiple_of(at, LANES), wide)
        value = jnp.dot(advection, hot[:, here], preferred_element_type=F32)
        high = lax.shift_right_arithmetic(slots[:, here], SHIFT)
        acc = jnp.zeros((values, wide), F32)
        for h in range(high_count):
            acc = jnp.where(high == h, value[h * values : (h + 1) * values], acc)
        return acc

    def collect_half(half, handle):
        slot = blocks.slot
        many = wide // slot

        def tail_step(n, _):
            value = collect(half * blocks.half + blocks.main + n * wide)
            for d in range(many):
                tails[n * many + d] = blocks.lanes(
                    [
                        value[g * 8 : g * 8 + 8, d * slot : (d + 1) * slot]
                        for g in range(blocks.groups)
                    ]
                )
            return 0

        lax.fori_loop(0, ranks // many, tail_step, 0)

        if blocks.full:

            def main_step(n, _):
                turn = lax.rem(me // 2 + 1 + n, ranks // 2)
                value = collect(half * blocks.half + turn * wide)
                for u in range(2):
                    rank = turn * 2 + u
                    handle(
                        rank, blocks.join(value[:, u * LANES : (u + 1) * LANES], tails[rank])
                    )
                return 0

            lax.fori_loop(0, ranks // 2, main_step, 0)
        else:

            def rank_step(n, _):
                rank = lax.rem(me + 1 + n, ranks)
                handle(rank, blocks.join(None, tails[rank]))
                return 0

            lax.fori_loop(0, ranks, rank_step, 0)

    def pair_back(rank):
        return pltpu.make_async_remote_copy(
            src_ref=give.at[rank], dst_ref=other.at[rank],
            send_sem=pass2_sem.at[rank], recv_sem=got2_sem.at[rank],
            device_id=(me, 1 - lat), device_id_type=MESH,
        )

    def rank_back(rank, source):
        return pltpu.make_async_remote_copy(
            src_ref=total.at[rank], dst_ref=back.at[source],
            send_sem=send2_sem.at[rank], recv_sem=recv2_sem.at[source],
            device_id=(rank, lat), device_id_type=MESH,
        )

    def to_other(rank, block):
        give[rank] = block.astype(BF16)
        pair_back(rank).start()

    def to_owner(rank, block):
        pair_back(rank).wait_recv()
        total[rank] = (block + other[rank].astype(F32)).astype(BF16)

        @pl.when(rank != me)
        def _():
            rank_back(rank, me).start()

    collect_half(1 - lat, to_other)
    collect_half(lat, to_owner)
    back[me] = total[me]

    def sent(d, _):
        rank = lax.rem(me + d, ranks)
        to_rank(rank, me).wait_send()
        to_pair(rank, lat).wait_send()
        pair_back(rank).wait_send()
        return 0

    lax.fori_loop(1, ranks, sent, 0)
    to_pair(me, lat).wait_send()
    pair_back(me).wait_send()
    keep.wait()

    def arrived(d, _):
        source = lax.rem(me + ranks - d, ranks)
        rank_back(source, source).wait_recv()
        return 0

    lax.fori_loop(1, ranks, arrived, 0)

    edge = 8
    held[:, 0:edge, :] = jnp.zeros((items, edge, columns), F32)
    held[:, edge + depth : 2 * edge + depth, :] = jnp.zeros((items, edge, columns), F32)
    for rank in range(ranks):
        value = back[rank].astype(F32)
        tail = jnp.concatenate(
            [
                value[base : base + 8, g * blocks.slot : g * blocks.slot + blocks.tail]
                for g in range(blocks.groups)
            ],
            0,
        )
        at = edge + rank * levels
        for item in range(items):
            here = slice(item * levels, (item + 1) * levels)
            if blocks.full:
                held[item, at : at + levels, 0:LANES] = value[here]
            held[item, at : at + levels, blocks.full * LANES : columns] = tail[here]

    scale = spacing[...]
    for item in range(items):

        def shifted(n):
            return held[item, edge + n : edge + n + depth, :]

        slant = shifted(-2) - 8.0 * shifted(-1) + 8.0 * shifted(1) - shifted(2)
        out[item] = shifted(0) + scale * slant

    def sent_back(d, _):
        rank_back(lax.rem(me + d, ranks), me).wait_send()
        return 0

    lax.fori_loop(1, ranks, sent_back, 0)


def body(
    forcing,
    pivots,
    lower,
    upper,
    slab_modes,
    slot_of_column,
    legendre,
    cycle_weight,
    zonal_flow,
    inverse_spacing,
):
    ranks, halves = lax.axis_size("rad"), lax.axis_size("lat")
    columns, depth = forcing.shape[2], forcing.shape[3]
    modes, degrees, cycles = legendre.shape
    levels = zonal_flow.shape[0]
    items = 6
    values = items * levels
    blocks = Blocks(columns, values, ranks)
    line = (ranks, blocks.rows, LANES)
    total = halves * blocks.half
    matrices = [m.transpose(1, 2, 3, 0) for m in (pivots, lower, upper)]
    right = forcing.transpose(0, 1, 3, 2).reshape(items, depth, columns)
    sizes = [right, *matrices, zonal_flow, legendre]

    solved, explicit = pl.pallas_call(
        functools.partial(kernel, blocks, halves),
        out_shape=(jax.ShapeDtypeStruct((items, depth, columns), F32),) * 2,
        in_specs=[SMEM] + [VMEM] * 3 + [ANY] * 6,
        out_specs=(ANY, VMEM),
        scratch_shapes=[pltpu.VMEM(x.shape, x.dtype) for x in sizes]
        + [
            pltpu.VMEM((items, depth, columns), F32),
            pltpu.VMEM((ranks, values, columns), F32),
            pltpu.VMEM(line, BF16),
            pltpu.VMEM((halves,) + line, BF16),
            pltpu.VMEM((LOW, total), BF16),
            pltpu.VMEM((modes * (degrees // LOW) * values, total), BF16),
            pltpu.VMEM((cycles // LANES, 2 * modes * 8 * 8, LANES), F32),
            pltpu.VMEM((modes, values, cycles), F32),
            pltpu.VMEM((modes, values, cycles), F32),
            pltpu.VMEM((ranks, 8, LANES), F32),
            pltpu.VMEM(line, BF16),
            pltpu.VMEM(line, BF16),
            pltpu.VMEM(line, BF16),
            pltpu.VMEM(line, BF16),
            pltpu.VMEM((items, depth + 16, columns), F32),
            pltpu.SemaphoreType.DMA((6,)),
            pltpu.SemaphoreType.DMA,
        ]
        + [pltpu.SemaphoreType.DMA((ranks,))] * 8,
        compiler_params=pltpu.CompilerParams(
            vmem_limit_bytes=ROOM, collective_id=0, has_side_effects=True
        ),
        name="step",
    )(
        slab_modes, blocks.order(slot_of_column, halves), inverse_spacing[:, None],
        cycle_weight[None], right, *matrices, zonal_flow, legendre,
    )

    def placed(value):
        return value.reshape(3, 2, depth, columns).transpose(0, 1, 3, 2)

    return (placed(solved), placed(explicit))


def solution(mesh):
    placed = (
        P(None, None, ("rad", "lat"), None),
        P(("rad", "lat"), None, None, None),
        P(("rad", "lat"), None, None, None),
        P(("rad", "lat"), None, None, None),
        P(),
        P(),
        P(None, None, "lat"),
        P("lat"),
        P("rad", "lat", None),
        P(),
    )
    return jax.shard_map(
        body,
        mesh=mesh,
        in_specs=placed,
        out_specs=(P(None, None, ("rad", "lat"), None), P(None, None, ("rad", "lat"), None)),
        check_vma=False,
    )
```

time: 420 us -> 42 us (0.10)
  local copies, waits for them, and re-layouts: 282 us -> 7.73 us
  matrix products: 36.6 us -> 0 us
  Pallas kernels: 0 us -> 33.3 us
  blocking collectives: 32.9 us -> 0 us
  waiting for transfers between devices: 25.4 us -> 0 us
  between operations: 14.6 us -> 0.67 us
  starting transfers between devices: 13.3 us -> 0 us
  other arithmetic: 11.4 us -> 0.01 us
    gather x5 -> x0, local copies, waits for them, and re-layouts: 175 us -> none  [the longest x2 75.8 us: body(): jnp.take(partial_value.reshape(item_count, 2, levels, slot_count), slot_a...]
    dot_general x7 -> x0, matrix products: 36.6 us -> none  [the longest x4 19.3 us: apply_block(): return jnp.einsum('kij,fckj->fcki', matrix, vector, precision=highest)]
    pallas_call x0 -> x1, Pallas kernels: none -> 33.3 us  [body(): pl.pallas_call(functools.partial(kernel, blocks, halves), out_shape=(jax....]
    unnamed x23 -> x3, local copies, waits for them, and re-layouts: 32.1 us -> 4.18 us
    psum x1 -> x0, waiting for transfers between devices: 20 us -> none  [body(): summed = lax.psum(partial_value, 'lat')]
    scatter x1 -> x0, local copies, waits for them, and re-layouts: 19.3 us -> none  [body(): pos_of_slot = jnp.zeros((slot_count,), jnp.int32).at[slot_at].set(positions)]
    all_to_all x5 -> x0, local copies, waits for them, and re-layouts: 17.6 us -> none  [the longest x3 10.6 us: body(): lax.all_to_all(explicit_part, 'rad', split_axis=3, concat_axis=2, tiled=T...]
    all_gather x1 -> x0, blocking collectives: 17.2 us -> none  [body(): lax.all_gather(lax.all_to_all(level_major, 'rad', split_axis=2, concat_ax...]
  transfers between devices with their start and end apart: 4 -> 0, of which waited for: 3 -> 0; matrix products, arithmetic and copies ran while one was open for 14% -> 0% of each run, Pallas kernels for 0% -> 0%
where the time goes in v2:
time: 42 us; the launch traced here: 41.7 us
  Pallas kernels  33.3 us (79%)
  local copies, waits for them, and re-layouts  7.73 us (18%)
  between operations  0.67 us (2%)
    pallas_call x1, Pallas kernels, body(): pl.pallas_call(functools.partial(kernel, blocks, halves), out_shape=(jax....  33.3 us
    unnamed x3, local copies, waits for them, and re-layouts  4.18 us
    broadcast_in_dim x1, local copies, waits for them, and re-layouts, body(): inverse_spacing[:, None]  1.36 us
    broadcast_in_dim x1, local copies, waits for them, and re-layouts, body(): cycle_weight[None]  1.27 us

profile of v2, /device:TPU:0, one launch (start us, length us, event | category | flops | bytes accessed | tf_op | source)
XLA Modules:
  0.0 41.7 jit_solution(9928447356531476201)
XLA Ops:
  0.6 1.3 %broadcast_in_dim.7.weight = f32[1,384]{1,0:T(1,128)} reshape(f32[384]{0:T(512)} %param.17) | data formatting | bytes 3072 | tf_op jit(solution)/shard_map/broadcast_in_dim | solution.py:549
  1.9 0.8 %reshape.25 = s32[16,2,160]{2,1,0:T(2,128)S(1)} reshape(s32[5120]{0:T(1024)} %param.15) | data formatting | bytes 40960 | tf_op jit(solution)/shard_map/reshape | solution.py:62
  2.8 0.1 reshape.27
  2.9 0.6 %copy.16 = s32[1,1,2,2560]{3,1,2,0:T(1,128)} copy(s32[1,1,2,2560]{3,2,1,0:T(2,128)S(1)} %add_bitcast_fusion) | data formatting | bytes 40960
  3.5 1.4 %copy.15.spacing = f32[64,1]{1,0:T(8,128)} copy(f32[64,1]{0,1:T(1,128)} %bitcast.29) | data formatting | bytes 512 | tf_op jit(solution)/shard_map/broadcast_in_dim | solution.py:548
  4.8 33.3 %step.1 = (f32[6,64,160]{2,1,0:T(8,128)}, f32[6,64,160]{2,1,0:T(8,128)}) custom-call(s32[5]{0:T(128)} %modes_ref.1, s32[1,5120]{1,0:T(1,128)} %bitcast.28, f32[64,1]{1,0:T(8,128)} %copy.15.spacing, f32[1,384]{1,0:T(1,128)} %broadcast_in_dim.7.weight, f32[6,64,160]{2,1,0:T(8,128)} %bitcast.25, f32[2,32,32,160]{3,2,1,0:T(8,128)} %bitcast.20, ...), custom_call_target="tpu_custom_call" | custom-call | tf_op jit(solution)/shard_map/step/pallas_call | solution.py:517
  38.1 1.8 %copy.19 = f32[3,2,160,64]{2,3,1,0:T(8,128)} copy(f32[3,2,160,64]{2,3,1,0:T(8,128)} %bitcast.24) | data formatting | bytes 491520
  39.9 1.8 %copy.20 = f32[3,2,160,64]{2,3,1,0:T(8,128)} copy(f32[3,2,160,64]{2,3,1,0:T(8,128)} %bitcast.23) | data formatting | bytes 491520
  (4 shorter events, 0.0 us)

commit v3 on v2

--- a/solution.py
+++ b/solution.py
@@ -58,14 +58,24 @@
         tail = self.lanes([rest[8 * g : 8 * g + 8] for g in range(self.groups)])
         return self.join(value[:, : self.full * LANES], tail)
 
-    def order(self, per_column, halves):
-        table = per_column.reshape(self.ranks, halves, self.columns).transpose(1, 0, 2)
-        main = table[:, :, : self.full * LANES].reshape(halves, self.main)
-        tail = table[:, :, self.full * LANES :]
-        tail = jnp.pad(
-            tail, ((0, 0), (0, 0), (0, self.slot - self.tail)), constant_values=-1
-        ).reshape(halves, self.ranks * self.slot)
-        return jnp.concatenate([main, tail], 1).reshape(1, halves * self.half)
+    def order(self, raw, halves, slots):
+        table = raw[...][None, :]
+        for half in range(halves):
+            for rank in range(self.ranks):
+                at = (rank * halves + half) * self.columns
+                if self.full:
+                    here = half * self.half + rank * LANES
+                    slots[:, here : here + LANES] = table[:, at : at + LANES]
+                    at += LANES
+            for first in range(0, self.ranks, self.share):
+                parts = []
+                for rank in range(first, first + self.share):
+                    at = (rank * halves + half) * self.columns + self.full * LANES
+                    parts.append(table[:, at : at + self.tail])
+                    if self.slot > self.tail:
+                        parts.append(jnp.full((1, self.slot - self.tail), -1, jnp.int32))
+                here = half * self.half + self.main + first * self.slot
+                slots[:, here : here + LANES] = jnp.concatenate(parts, 1)
 
 
 def sublane_sums(values):
@@ -83,10 +93,10 @@
 
 
 def kernel(
-    blocks, halves, modes_ref, slots, spacing, weight, forcing_hbm, pivots_hbm, lower_hbm,
-    upper_hbm, zonal_hbm, legendre_hbm, solved_hbm, out,
-    forcing, pivots, lower, upper, zonal, legendre, solved, stage, send, message, hot, spread,
-    waves, spectral, turned, tails, give, other, total, back, held,
+    blocks, halves, modes_ref, raw_slots, weight, forcing_hbm, pivots_hbm, lower_hbm,
+    upper_hbm, zonal_hbm, legendre_hbm, solved_hbm, back,
+    slots, forcing, pivots, lower, upper, zonal, legendre, solved, stage, send, message, hot, spread,
+    waves, spectral, turned, tails, give, other, total,
     load_sem, solved_sem, send_sem, recv_sem, pass_sem, got_sem,
     send2_sem, recv2_sem, pass2_sem, got2_sem,
 ):
@@ -110,7 +120,7 @@
             )
         )
     ]
-    for load in loads:
+    for load in loads[:4]:
         load.start()
 
     barrier = pltpu.get_barrier_semaphore()
@@ -180,6 +190,7 @@
     for item in range(items):
         solved[item, span(0)] = first[item]
     loads[2].wait()
+    loads[4].start()
 
     def descend(k, carry):
         drop = apply_block(lower, k - 1, carry)
@@ -217,6 +228,7 @@
     to_pair(me, lat).start()
 
     loads[4].wait()
+    loads[5].start()
     row = lax.broadcasted_iota(jnp.int32, (8, phi_count), 0)
     column = lax.broadcasted_iota(jnp.int32, (8, phi_count), 1).astype(F32)
     wave = jnp.zeros((8, phi_count), F32)
@@ -286,6 +298,8 @@
 
     lax.fori_loop(1, ranks, hand_on, 0)
 
+    blocks.order(raw_slots, halves, slots)
+
     def heat(n, _):
         here = pl.ds(pl.multiple_of(n * LANES, LANES), LANES)
         low = slots[:, here] & (LOW - 1)
@@ -345,7 +359,7 @@
                         acc = term if acc is None else acc + term
                 parts.append(acc)
             stack.append(jnp.concatenate(parts, 1))
-        sums.append((jnp.concatenate(stack, 0) * weight[...]).astype(BF16))
+        sums.append((jnp.concatenate(stack, 0) * weight[...][None, :]).astype(BF16))
 
     pieces = []
     for i in range(modes):
@@ -454,6 +468,19 @@
 
     lax.fori_loop(1, ranks, arrived, 0)
 
+    def sent_back(d, _):
+        rank_back(lax.rem(me + d, ranks), me).wait_send()
+        return 0
+
+    lax.fori_loop(1, ranks, sent_back, 0)
+
+
+def last_kernel(blocks, spacing, back, solved, solved_out, out, held, solved_sem):
+    ranks, values, base = blocks.ranks, blocks.values, blocks.base
+    items, depth, columns = out.shape
+    levels = depth // ranks
+    hand_on = pltpu.make_async_copy(solved, solved_out, solved_sem)
+    hand_on.start()
     edge = 8
     held[:, 0:edge, :] = jnp.zeros((items, edge, columns), F32)
     held[:, edge + depth : 2 * edge + depth, :] = jnp.zeros((items, edge, columns), F32)
@@ -473,7 +500,10 @@
                 held[item, at : at + levels, 0:LANES] = value[here]
             held[item, at : at + levels, blocks.full * LANES : columns] = tail[here]
 
-    scale = spacing[...]
+    keep = lax.broadcasted_iota(jnp.int32, (depth, depth), 0) == lax.broadcasted_iota(
+        jnp.int32, (depth, depth), 1
+    )
+    scale = jnp.sum(jnp.where(keep, spacing[...][None, :], 0.0), axis=1, keepdims=True)
     for item in range(items):
 
         def shifted(n):
@@ -482,11 +512,7 @@
         slant = shifted(-2) - 8.0 * shifted(-1) + 8.0 * shifted(1) - shifted(2)
         out[item] = shifted(0) + scale * slant
 
-    def sent_back(d, _):
-        rank_back(lax.rem(me + d, ranks), me).wait_send()
-        return 0
-
-    lax.fori_loop(1, ranks, sent_back, 0)
+    hand_on.wait()
 
 
 def body(
@@ -514,12 +540,15 @@
     right = forcing.transpose(0, 1, 3, 2).reshape(items, depth, columns)
     sizes = [right, *matrices, zonal_flow, legendre]
 
-    solved, explicit = pl.pallas_call(
+    grid = jax.ShapeDtypeStruct((items, depth, columns), F32)
+
+    solved, back = pl.pallas_call(
         functools.partial(kernel, blocks, halves),
-        out_shape=(jax.ShapeDtypeStruct((items, depth, columns), F32),) * 2,
-        in_specs=[SMEM] + [VMEM] * 3 + [ANY] * 6,
+        out_shape=(grid, jax.ShapeDtypeStruct(line, BF16)),
+        in_specs=[SMEM] + [VMEM] * 2 + [ANY] * 6,
         out_specs=(ANY, VMEM),
-        scratch_shapes=[pltpu.VMEM(x.shape, x.dtype) for x in sizes]
+        scratch_shapes=[pltpu.VMEM((1, total), jnp.int32)]
+        + [pltpu.VMEM(x.shape, x.dtype) for x in sizes]
         + [
             pltpu.VMEM((items, depth, columns), F32),
             pltpu.VMEM((ranks, values, columns), F32),
@@ -534,8 +563,6 @@
             pltpu.VMEM(line, BF16),
             pltpu.VMEM(line, BF16),
             pltpu.VMEM(line, BF16),
-            pltpu.VMEM(line, BF16),
-            pltpu.VMEM((items, depth + 16, columns), F32),
             pltpu.SemaphoreType.DMA((6,)),
             pltpu.SemaphoreType.DMA,
         ]
@@ -544,10 +571,20 @@
             vmem_limit_bytes=ROOM, collective_id=0, has_side_effects=True
         ),
         name="step",
-    )(
-        slab_modes, blocks.order(slot_of_column, halves), inverse_spacing[:, None],
-        cycle_weight[None], right, *matrices, zonal_flow, legendre,
-    )
+    )(slab_modes, slot_of_column, cycle_weight, right, *matrices, zonal_flow, legendre)
+
+    solved, explicit = pl.pallas_call(
+        functools.partial(last_kernel, blocks),
+        out_shape=(grid, grid),
+        in_specs=[VMEM, VMEM, ANY],
+        out_specs=(ANY, VMEM),
+        scratch_shapes=[
+            pltpu.VMEM((items, depth + 16, columns), F32),
+            pltpu.SemaphoreType.DMA,
+        ],
+        compiler_params=pltpu.CompilerParams(vmem_limit_bytes=ROOM),
+        name="stencil",
+    )(inverse_spacing, back, solved)
 
     def placed(value):
         return value.reshape(3, 2, depth, columns).transpose(0, 1, 3, 2)

time: 42 us -> 48.4 us (1.15)
  Pallas kernels: 33.3 us -> 47.6 us
  local copies, waits for them, and re-layouts: 7.73 us -> 0 us
    pallas_call x1 -> x2, Pallas kernels: 33.3 us -> 47.6 us  [the longest x1 32.9 us: body(): pl.pallas_call(functools.partial(kernel, blocks, halves), out_shape=(grid...]
    unnamed x3 -> x0, local copies, waits for them, and re-layouts: 4.18 us -> none
    broadcast_in_dim x2 -> x0, local copies, waits for them, and re-layouts: 2.63 us -> none  [the longest x1 1.36 us: body(): inverse_spacing[:, None]]
    reshape x3 -> x0, local copies, waits for them, and re-layouts: 0.91 us -> none  [the longest x1 0.82 us: order(): per_column.reshape(self.ranks, halves, self.columns).transpose(1, 0, 2)]
where the time goes in v3:
time: 48.4 us; the launch traced here: 48.2 us
  Pallas kernels  47.6 us (98%)
  between operations  0.64 us (1%)
    pallas_call x1, Pallas kernels, body(): pl.pallas_call(functools.partial(kernel, blocks, halves), out_shape=(grid...  32.9 us
    pallas_call x1, Pallas kernels, body(): pl.pallas_call(functools.partial(last_kernel, blocks), out_shape=(grid, g...  14.7 us

profile of v3, /device:TPU:0, one launch (start us, length us, event | category | flops | bytes accessed | tf_op | source)
XLA Modules:
  0.0 48.2 jit_solution(13510270286449090864)
XLA Ops:
  0.6 32.9 %step.1 = (f32[6,64,160]{2,1,0:T(8,128)}, bf16[16,32,128]{2,1,0:T(8,128)(2,1)}) custom-call(s32[5]{0:T(128)} %modes_ref.1, s32[5120]{0:T(1024)} %raw_slots.1, f32[384]{0:T(512)} %weight.1, f32[6,64,160]{2,1,0:T(8,128)} %bitcast.15, f32[2,32,32,160]{3,2,1,0:T(8,128)} %bitcast.12, f32[1,32,32,160]{3,2,1,0:T(8,128)} %bitcast.13, f32[1,32,32,160]{3,2,1,0:T(8,128)} %bitcast.14, ...), custom_call_target="tpu_custom_call" | custom-call | tf_op jit(solution)/shard_map/step/pallas_call | solution.py:545
  33.5 14.7 %stencil.1 = (f32[6,64,160]{2,1,0:T(8,128)}, f32[6,64,160]{2,1,0:T(8,128)}) custom-call(f32[64]{0:T(128)} %spacing.1, bf16[16,32,128]{2,1,0:T(8,128)(2,1)} %get-tuple-element.6.back, f32[6,64,160]{2,1,0:T(8,128)} %get-tuple-element.7.solved), custom_call_target="tpu_custom_call" | custom-call | tf_op jit(solution)/shard_map/stencil/pallas_call | solution.py:576

commit v4 on v3

--- a/solution.py
+++ b/solution.py
@@ -111,17 +111,18 @@
     high_count = modes * chunks
     fields = values // 8
 
-    loads = [
-        pltpu.make_async_copy(source, target, load_sem.at[n])
-        for n, (source, target) in enumerate(
-            (
-                (forcing_hbm, forcing), (pivots_hbm, pivots), (lower_hbm, lower),
-                (upper_hbm, upper), (zonal_hbm, zonal), (legendre_hbm, legendre),
-            )
-        )
-    ]
-    for load in loads[:4]:
-        load.start()
+    def load(n, source, target):
+        return pltpu.make_async_copy(source, target, load_sem.at[n])
+
+    load_right = load(0, forcing_hbm, forcing)
+    load_first = load(1, pivots_hbm.at[0], pivots.at[0])
+    load_rest = load(2, pivots_hbm.at[pl.ds(1, count - 1)], pivots.at[pl.ds(1, count - 1)])
+    load_lower = load(3, lower_hbm, lower)
+    load_upper = load(4, upper_hbm, upper)
+    load_zonal = load(5, zonal_hbm, zonal)
+    load_legendre = load(6, legendre_hbm, legendre)
+    for one in (load_right, load_first, load_lower, load_rest, load_upper):
+        one.start()
 
     barrier = pltpu.get_barrier_semaphore()
     pl.semaphore_signal(barrier, inc=1, device_id=(me, 1 - lat), device_id_type=MESH)
@@ -184,13 +185,14 @@
 
         lax.fori_loop(0, per_block, give_one, 0)
 
-    loads[0].wait()
-    loads[1].wait()
+    load_right.wait()
+    load_first.wait()
     first = apply_block(pivots, 0, [forcing[item, span(0)] for item in range(items)])
     for item in range(items):
         solved[item, span(0)] = first[item]
-    loads[2].wait()
-    loads[4].start()
+    load_lower.wait()
+    load_rest.wait()
+    load_zonal.start()
 
     def descend(k, carry):
         drop = apply_block(lower, k - 1, carry)
@@ -205,7 +207,7 @@
         last = descend(1, last)
     else:
         last = lax.fori_loop(1, count, descend, last)
-    loads[3].wait()
+    load_upper.wait()
     pl.semaphore_wait(barrier, ranks)
     emit(count - 1, last)
 
@@ -227,8 +229,8 @@
     message[lat, me] = send[me]
     to_pair(me, lat).start()
 
-    loads[4].wait()
-    loads[5].start()
+    load_zonal.wait()
+    load_legendre.start()
     row = lax.broadcasted_iota(jnp.int32, (8, phi_count), 0)
     column = lax.broadcasted_iota(jnp.int32, (8, phi_count), 1).astype(F32)
     wave = jnp.zeros((8, phi_count), F32)
@@ -252,7 +254,8 @@
     tables = jnp.concatenate([high, rest], 0)
     across = (((1,), (1,)), ((), ()))
     pairs = 2 * modes * 8
-    for r in range(levels):
+
+    def azimuth(r):
         value = lax.dot_general(tables, zonal[r], across, preferred_element_type=F32)
         value = value[: 2 * pairs] + value[2 * pairs :]
         for c in range(2):
@@ -260,6 +263,19 @@
                 waves[part, pl.ds(c * levels + r, pairs, stride=8), :] = value[
                     c * pairs : (c + 1) * pairs, part * LANES : (part + 1) * LANES
                 ]
+
+    for r in range(levels // 2):
+        azimuth(r)
+    blocks.order(raw_slots, halves, slots)
+
+    def heat(n, _):
+        here = pl.ds(pl.multiple_of(n * LANES, LANES), LANES)
+        low = slots[:, here] & (LOW - 1)
+        rows = lax.broadcasted_iota(jnp.int32, (LOW, LANES), 0)
+        hot[:, here] = jnp.where(rows == low, 1.0, 0.0).astype(BF16)
+        return 0
+
+    lax.fori_loop(0, halves * blocks.half // LANES, heat, 0)
 
     def lay(at, value):
         here = pl.ds(pl.multiple_of(at, LANES), LANES)
@@ -298,16 +314,8 @@
 
     lax.fori_loop(1, ranks, hand_on, 0)
 
-    blocks.order(raw_slots, halves, slots)
-
-    def heat(n, _):
-        here = pl.ds(pl.multiple_of(n * LANES, LANES), LANES)
-        low = slots[:, here] & (LOW - 1)
-        rows = lax.broadcasted_iota(jnp.int32, (LOW, LANES), 0)
-        hot[:, here] = jnp.where(rows == low, 1.0, 0.0).astype(BF16)
-        return 0
-
-    lax.fori_loop(0, halves * blocks.half // LANES, heat, 0)
+    for r in range(levels // 2, levels):
+        azimuth(r)
 
     def mine(source, _):
         lay_main(lat, source)
@@ -330,7 +338,7 @@
     def allowed(i, n):
         return lane + n * LOW >= modes_ref[i]
 
-    loads[5].wait()
+    load_legendre.wait()
     for i in range(modes):
         rows = []
         for n in range(chunks):
@@ -369,7 +377,7 @@
             pieces.append(jnp.where(allowed(i, n), piece, 0.0))
     advection = jnp.concatenate(pieces, 0).astype(BF16)
 
-    wide = 2 * LANES
+    wide = 4 * LANES
 
     def collect(at):
         here = pl.ds(pl.multiple_of(at, LANES), wide)
@@ -400,16 +408,16 @@
         if blocks.full:
 
             def main_step(n, _):
-                turn = lax.rem(me // 2 + 1 + n, ranks // 2)
+                turn = lax.rem(me // 4 + 1 + n, ranks // 4)
                 value = collect(half * blocks.half + turn * wide)
-                for u in range(2):
-                    rank = turn * 2 + u
+                for u in range(4):
+                    rank = turn * 4 + u
                     handle(
                         rank, blocks.join(value[:, u * LANES : (u + 1) * LANES], tails[rank])
                     )
                 return 0
 
-            lax.fori_loop(0, ranks // 2, main_step, 0)
+            lax.fori_loop(0, ranks // 4, main_step, 0)
         else:
 
             def rank_step(n, _):
@@ -475,12 +483,21 @@
     lax.fori_loop(1, ranks, sent_back, 0)
 
 
-def last_kernel(blocks, spacing, back, solved, solved_out, out, held, solved_sem):
+def last_kernel(
+    blocks, spacing, back, solved, solved_out, out, held, passing, load_sem, solved_sem
+):
     ranks, values, base = blocks.ranks, blocks.values, blocks.base
     items, depth, columns = out.shape
     levels = depth // ranks
-    hand_on = pltpu.make_async_copy(solved, solved_out, solved_sem)
-    hand_on.start()
+
+    def load(item):
+        return pltpu.make_async_copy(solved.at[item], passing.at[item], load_sem.at[item])
+
+    def leave(item):
+        return pltpu.make_async_copy(passing.at[item], solved_out.at[item], solved_sem.at[item])
+
+    for item in range(items):
+        load(item).start()
     edge = 8
     held[:, 0:edge, :] = jnp.zeros((items, edge, columns), F32)
     held[:, edge + depth : 2 * edge + depth, :] = jnp.zeros((items, edge, columns), F32)
@@ -500,6 +517,9 @@
                 held[item, at : at + levels, 0:LANES] = value[here]
             held[item, at : at + levels, blocks.full * LANES : columns] = tail[here]
 
+    for item in range(items):
+        load(item).wait()
+        leave(item).start()
     keep = lax.broadcasted_iota(jnp.int32, (depth, depth), 0) == lax.broadcasted_iota(
         jnp.int32, (depth, depth), 1
     )
@@ -512,7 +532,8 @@
         slant = shifted(-2) - 8.0 * shifted(-1) + 8.0 * shifted(1) - shifted(2)
         out[item] = shifted(0) + scale * slant
 
-    hand_on.wait()
+    for item in range(items):
+        leave(item).wait()
 
 
 def body(
@@ -563,7 +584,7 @@
             pltpu.VMEM(line, BF16),
             pltpu.VMEM(line, BF16),
             pltpu.VMEM(line, BF16),
-            pltpu.SemaphoreType.DMA((6,)),
+            pltpu.SemaphoreType.DMA((7,)),
             pltpu.SemaphoreType.DMA,
         ]
         + [pltpu.SemaphoreType.DMA((ranks,))] * 8,
@@ -580,7 +601,9 @@
         out_specs=(ANY, VMEM),
         scratch_shapes=[
             pltpu.VMEM((items, depth + 16, columns), F32),
-            pltpu.SemaphoreType.DMA,
+            pltpu.VMEM((items, depth, columns), F32),
+            pltpu.SemaphoreType.DMA((items,)),
+            pltpu.SemaphoreType.DMA((items,)),
         ],
         compiler_params=pltpu.CompilerParams(vmem_limit_bytes=ROOM),
         name="stencil",

time: 48.4 us -> 35.5 us (0.73)
  Pallas kernels: 47.6 us -> 34.6 us
    pallas_call x1, Pallas kernels: 14.7 us -> 3.41 us  [body(): pl.pallas_call(functools.partial(last_kernel, blocks), out_shape=(grid, g...]
    pallas_call x1, Pallas kernels: 32.9 us -> 31.2 us  [body(): pl.pallas_call(functools.partial(kernel, blocks, halves), out_shape=(grid...]
where the time goes in v4:
time: 35.5 us; the launch traced here: 35.3 us
  Pallas kernels  34.6 us (97%)
  between operations  0.64 us (2%)
    pallas_call x1, Pallas kernels, body(): pl.pallas_call(functools.partial(kernel, blocks, halves), out_shape=(grid...  31.2 us
    pallas_call x1, Pallas kernels, body(): pl.pallas_call(functools.partial(last_kernel, blocks), out_shape=(grid, g...  3.41 us

profile of v4, /device:TPU:0, one launch (start us, length us, event | category | flops | bytes accessed | tf_op | source)
XLA Modules:
  0.0 35.3 jit_solution(7984339069901945584)
XLA Ops:
  0.6 31.2 %step.1 = (f32[6,64,160]{2,1,0:T(8,128)}, bf16[16,32,128]{2,1,0:T(8,128)(2,1)}) custom-call(s32[5]{0:T(128)} %modes_ref.1, s32[5120]{0:T(1024)} %raw_slots.1, f32[384]{0:T(512)} %weight.1, f32[6,64,160]{2,1,0:T(8,128)} %bitcast.15, f32[2,32,32,160]{3,2,1,0:T(8,128)} %bitcast.12, f32[1,32,32,160]{3,2,1,0:T(8,128)} %bitcast.13, f32[1,32,32,160]{3,2,1,0:T(8,128)} %bitcast.14, ...), custom_call_target="tpu_custom_call" | custom-call | tf_op jit(solution)/shard_map/step/pallas_call | solution.py:566
  31.9 3.4 %stencil.1 = (f32[6,64,160]{2,1,0:T(8,128)}, f32[6,64,160]{2,1,0:T(8,128)}) custom-call(f32[64]{0:T(128)} %spacing.1, bf16[16,32,128]{2,1,0:T(8,128)(2,1)} %get-tuple-element.6.back, f32[6,64,160]{2,1,0:T(8,128)} %get-tuple-element.7.solved), custom_call_target="tpu_custom_call" | custom-call | tf_op jit(solution)/shard_map/stencil/pallas_call | solution.py:597

commit v5 on v4

--- a/solution.py
+++ b/solution.py
@@ -14,10 +14,10 @@
 MESH = pl.DeviceIdType.MESH
 VMEM = pl.BlockSpec(memory_space=pltpu.VMEM)
 SMEM = pl.BlockSpec(memory_space=pltpu.SMEM)
-ANY = pl.BlockSpec(memory_space=pl.ANY)
+HBM = pl.BlockSpec(memory_space=pltpu.HBM)
 F32 = jnp.float32
 BF16 = jnp.bfloat16
-ROOM = 60 * 1024 * 1024
+MIB = 1024 * 1024
 
 
 class Blocks:
@@ -93,11 +93,11 @@
 
 
 def kernel(
-    blocks, halves, modes_ref, raw_slots, weight, forcing_hbm, pivots_hbm, lower_hbm,
-    upper_hbm, zonal_hbm, legendre_hbm, solved_hbm, back,
-    slots, forcing, pivots, lower, upper, zonal, legendre, solved, stage, send, message, hot, spread,
-    waves, spectral, turned, tails, give, other, total,
-    load_sem, solved_sem, send_sem, recv_sem, pass_sem, got_sem,
+    blocks, halves, modes_ref, slots_hbm, weight_hbm, forcing_hbm, pivots_hbm, lower_hbm,
+    upper_hbm, zonal_hbm, legendre_hbm, solved, back,
+    raw_slots, weight, slots, forcing, pivots, lower, upper, zonal, legendre, stage, send, message, hot, spread,
+    waves, spectral, turned, tails, give, other, total, tables,
+    load_sem, send_sem, recv_sem, pass_sem, got_sem,
     send2_sem, recv2_sem, pass2_sem, got2_sem,
 ):
     me, lat = lax.axis_index("rad"), lax.axis_index("lat")
@@ -121,8 +121,12 @@
     load_upper = load(4, upper_hbm, upper)
     load_zonal = load(5, zonal_hbm, zonal)
     load_legendre = load(6, legendre_hbm, legendre)
+    load_slots = load(7, slots_hbm, raw_slots)
+    load_weight = load(8, weight_hbm, weight)
     for one in (load_right, load_first, load_lower, load_rest, load_upper):
         one.start()
+    load_slots.start()
+    load_weight.start()
 
     barrier = pltpu.get_barrier_semaphore()
     pl.semaphore_signal(barrier, inc=1, device_id=(me, 1 - lat), device_id_type=MESH)
@@ -185,52 +189,6 @@
 
         lax.fori_loop(0, per_block, give_one, 0)
 
-    load_right.wait()
-    load_first.wait()
-    first = apply_block(pivots, 0, [forcing[item, span(0)] for item in range(items)])
-    for item in range(items):
-        solved[item, span(0)] = first[item]
-    load_lower.wait()
-    load_rest.wait()
-    load_zonal.start()
-
-    def descend(k, carry):
-        drop = apply_block(lower, k - 1, carry)
-        rest = [forcing[item, span(k)] - drop[item] for item in range(items)]
-        now = apply_block(pivots, k, rest)
-        for item in range(items):
-            solved[item, span(k)] = now[item]
-        return tuple(now)
-
-    last = tuple(first)
-    if count == 2:
-        last = descend(1, last)
-    else:
-        last = lax.fori_loop(1, count, descend, last)
-    load_upper.wait()
-    pl.semaphore_wait(barrier, ranks)
-    emit(count - 1, last)
-
-    def up_step(step, carry):
-        k = count - 2 - step
-        drop = apply_block(upper, k, carry)
-        now = [solved[item, span(k)] - drop[item] for item in range(items)]
-        for item in range(items):
-            solved[item, span(k)] = now[item]
-        emit(k, now)
-        return tuple(now)
-
-    if count == 2:
-        up_step(0, last)
-    else:
-        lax.fori_loop(0, count - 1, up_step, last)
-    keep = pltpu.make_async_copy(solved, solved_hbm, solved_sem)
-    keep.start()
-    message[lat, me] = send[me]
-    to_pair(me, lat).start()
-
-    load_zonal.wait()
-    load_legendre.start()
     row = lax.broadcasted_iota(jnp.int32, (8, phi_count), 0)
     column = lax.broadcasted_iota(jnp.int32, (8, phi_count), 1).astype(F32)
     wave = jnp.zeros((8, phi_count), F32)
@@ -249,23 +207,69 @@
             for i in range(modes):
                 rows.append(slope[c if e == 0 else 1 - c][i : i + 1] * turn[c])
     table = jnp.concatenate(rows, 0)
-    high = table.astype(BF16)
-    rest = (table - high.astype(F32)).astype(BF16)
-    tables = jnp.concatenate([high, rest], 0)
+    tables[...] = table.astype(BF16)
+
+    load_right.wait()
+    load_first.wait()
+    first = apply_block(pivots, 0, [forcing[item, span(0)] for item in range(items)])
+    for item in range(items):
+        solved[item, span(0)] = first[item]
+    load_lower.wait()
+    load_rest.wait()
+    load_zonal.start()
+
+    def descend(k, carry):
+        drop = apply_block(lower, k - 1, carry)
+        rest = [forcing[item, span(k)] - drop[item] for item in range(items)]
+        now = apply_block(pivots, k, rest)
+        for item in range(items):
+            solved[item, span(k)] = now[item]
+        return tuple(now)
+
+    last = tuple(first)
+    if count == 2:
+        last = descend(1, last)
+    else:
+        last = lax.fori_loop(1, count, descend, last)
+    load_upper.wait()
+    pl.semaphore_wait(barrier, ranks)
+    emit(count - 1, last)
+
+    def up_step(step, carry):
+        k = count - 2 - step
+        drop = apply_block(upper, k, carry)
+        now = [solved[item, span(k)] - drop[item] for item in range(items)]
+        for item in range(items):
+            solved[item, span(k)] = now[item]
+        emit(k, now)
+        return tuple(now)
+
+    if count == 2:
+        up_step(0, last)
+    else:
+        lax.fori_loop(0, count - 1, up_step, last)
+    message[lat, me] = send[me]
+    to_pair(me, lat).start()
+
+    load_zonal.wait()
+    load_legendre.start()
     across = (((1,), (1,)), ((), ()))
     pairs = 2 * modes * 8
 
     def azimuth(r):
-        value = lax.dot_general(tables, zonal[r], across, preferred_element_type=F32)
-        value = value[: 2 * pairs] + value[2 * pairs :]
-        for c in range(2):
-            for part in range(cycles // LANES):
-                waves[part, pl.ds(c * levels + r, pairs, stride=8), :] = value[
-                    c * pairs : (c + 1) * pairs, part * LANES : (part + 1) * LANES
-                ]
-
-    for r in range(levels // 2):
+        flow = zonal[r : r + 2].reshape(2 * cycles, phi_count)
+        value = lax.dot_general(tables[...], flow, across, preferred_element_type=F32)
+        for u in range(2):
+            for c in range(2):
+                for part in range(cycles // LANES):
+                    at = u * cycles + part * LANES
+                    waves[part, pl.ds(c * levels + r + u, pairs, stride=8), :] = value[
+                        c * pairs : (c + 1) * pairs, at : at + LANES
+                    ]
+
+    for r in range(0, levels // 2, 2):
         azimuth(r)
+    load_slots.wait()
     blocks.order(raw_slots, halves, slots)
 
     def heat(n, _):
@@ -314,7 +318,7 @@
 
     lax.fori_loop(1, ranks, hand_on, 0)
 
-    for r in range(levels // 2, levels):
+    for r in range(levels // 2, levels, 2):
         azimuth(r)
 
     def mine(source, _):
@@ -339,6 +343,7 @@
         return lane + n * LOW >= modes_ref[i]
 
     load_legendre.wait()
+    load_weight.wait()
     for i in range(modes):
         rows = []
         for n in range(chunks):
@@ -467,7 +472,6 @@
     lax.fori_loop(1, ranks, sent, 0)
     to_pair(me, lat).wait_send()
     pair_back(me).wait_send()
-    keep.wait()
 
     def arrived(d, _):
         source = lax.rem(me + ranks - d, ranks)
@@ -484,20 +488,14 @@
 
 
 def last_kernel(
-    blocks, spacing, back, solved, solved_out, out, held, passing, load_sem, solved_sem
+    blocks, spacing, back, solved, solved_out, out, held, solved_sem
 ):
     ranks, values, base = blocks.ranks, blocks.values, blocks.base
     items, depth, columns = out.shape
     levels = depth // ranks
 
-    def load(item):
-        return pltpu.make_async_copy(solved.at[item], passing.at[item], load_sem.at[item])
-
-    def leave(item):
-        return pltpu.make_async_copy(passing.at[item], solved_out.at[item], solved_sem.at[item])
-
-    for item in range(items):
-        load(item).start()
+    hand_on = pltpu.make_async_copy(solved, solved_out, solved_sem)
+    hand_on.start()
     edge = 8
     held[:, 0:edge, :] = jnp.zeros((items, edge, columns), F32)
     held[:, edge + depth : 2 * edge + depth, :] = jnp.zeros((items, edge, columns), F32)
@@ -517,9 +515,6 @@
                 held[item, at : at + levels, 0:LANES] = value[here]
             held[item, at : at + levels, blocks.full * LANES : columns] = tail[here]
 
-    for item in range(items):
-        load(item).wait()
-        leave(item).start()
     keep = lax.broadcasted_iota(jnp.int32, (depth, depth), 0) == lax.broadcasted_iota(
         jnp.int32, (depth, depth), 1
     )
@@ -532,8 +527,7 @@
         slant = shifted(-2) - 8.0 * shifted(-1) + 8.0 * shifted(1) - shifted(2)
         out[item] = shifted(0) + scale * slant
 
-    for item in range(items):
-        leave(item).wait()
+    hand_on.wait()
 
 
 def body(
@@ -566,12 +560,15 @@
     solved, back = pl.pallas_call(
         functools.partial(kernel, blocks, halves),
         out_shape=(grid, jax.ShapeDtypeStruct(line, BF16)),
-        in_specs=[SMEM] + [VMEM] * 2 + [ANY] * 6,
-        out_specs=(ANY, VMEM),
-        scratch_shapes=[pltpu.VMEM((1, total), jnp.int32)]
+        in_specs=[SMEM] + [HBM] * 8,
+        out_specs=(VMEM, VMEM),
+        scratch_shapes=[
+            pltpu.VMEM(slot_of_column.shape, jnp.int32),
+            pltpu.VMEM(cycle_weight.shape, F32),
+            pltpu.VMEM((1, total), jnp.int32),
+        ]
         + [pltpu.VMEM(x.shape, x.dtype) for x in sizes]
         + [
-            pltpu.VMEM((items, depth, columns), F32),
             pltpu.VMEM((ranks, values, columns), F32),
             pltpu.VMEM(line, BF16),
             pltpu.VMEM((halves,) + line, BF16),
@@ -584,12 +581,12 @@
             pltpu.VMEM(line, BF16),
             pltpu.VMEM(line, BF16),
             pltpu.VMEM(line, BF16),
-            pltpu.SemaphoreType.DMA((7,)),
-            pltpu.SemaphoreType.DMA,
+            pltpu.VMEM((4 * modes * 8, zonal_flow.shape[2]), BF16),
+            pltpu.SemaphoreType.DMA((9,)),
         ]
         + [pltpu.SemaphoreType.DMA((ranks,))] * 8,
         compiler_params=pltpu.CompilerParams(
-            vmem_limit_bytes=ROOM, collective_id=0, has_side_effects=True
+            vmem_limit_bytes=(53 if total <= 8000 else 60) * MIB, collective_id=0, has_side_effects=True
         ),
         name="step",
     )(slab_modes, slot_of_column, cycle_weight, right, *matrices, zonal_flow, legendre)
@@ -597,15 +594,13 @@
     solved, explicit = pl.pallas_call(
         functools.partial(last_kernel, blocks),
         out_shape=(grid, grid),
-        in_specs=[VMEM, VMEM, ANY],
-        out_specs=(ANY, VMEM),
+        in_specs=[VMEM] * 3,
+        out_specs=(HBM, VMEM),
         scratch_shapes=[
             pltpu.VMEM((items, depth + 16, columns), F32),
-            pltpu.VMEM((items, depth, columns), F32),
-            pltpu.SemaphoreType.DMA((items,)),
-            pltpu.SemaphoreType.DMA((items,)),
+            pltpu.SemaphoreType.DMA,
         ],
-        compiler_params=pltpu.CompilerParams(vmem_limit_bytes=ROOM),
+        compiler_params=pltpu.CompilerParams(vmem_limit_bytes=16 * MIB),
         name="stencil",
     )(inverse_spacing, back, solved)
 

time: 35.5 us -> 35.8 us (level)
  local copies, waits for them, and re-layouts: 0 us -> 3.06 us
  Pallas kernels: 34.6 us -> 31.8 us
    unnamed x0 -> x10, local copies, waits for them, and re-layouts: none -> 3.06 us
    pallas_call x1, Pallas kernels: 3.41 us -> 1.53 us  [body(): pl.pallas_call(functools.partial(last_kernel, blocks), out_shape=(grid, g...]
    pallas_call x1, Pallas kernels: 31.2 us -> 30.3 us  [body(): pl.pallas_call(functools.partial(kernel, blocks, halves), out_shape=(grid...]
where the time goes in v5:
time: 35.8 us; the launch traced here: 35.5 us
  Pallas kernels  31.8 us (89%)
  local copies, waits for them, and re-layouts  3.06 us (9%)
  between operations  0.66 us (2%)
    pallas_call x1, Pallas kernels, body(): pl.pallas_call(functools.partial(kernel, blocks, halves), out_shape=(grid...  30.3 us
    unnamed x10, local copies, waits for them, and re-layouts  3.06 us
    pallas_call x1, Pallas kernels, body(): pl.pallas_call(functools.partial(last_kernel, blocks), out_shape=(grid, g...  1.53 us

profile of v5, /device:TPU:0, one launch (start us, length us, event | category | flops | bytes accessed | tf_op | source)
XLA Modules:
  0.0 35.5 jit_solution(8126963084865451268)
XLA Ops:
  0.6 0.0 copy-start
  0.6 1.0 %copy-done = f32[3,2,160,64]{2,3,1,0:T(8,128)S(1)} copy-done((f32[3,2,160,64]{2,3,1,0:T(8,128)S(1)}, f32[3,2,160,64]{2,3,1,0:T(8,128)}, u32[]{:S(2)}) %copy-start) | copy-done | bytes 245784
  1.6 0.0 copy-start.1
  1.6 0.7 %copy-done.1 = s32[5120]{0:T(1024)S(1)} copy-done((s32[5120]{0:T(1024)S(1)}, s32[5120]{0:T(1024)}, u32[]{:S(2)}) %copy-start.1) | copy-done | bytes 20504
  2.4 0.0 copy-start.2
  2.4 0.7 %copy-done.2 = f32[384]{0:T(512)S(1)} copy-done((f32[384]{0:T(512)S(1)}, f32[384]{0:T(512)}, u32[]{:S(2)}) %copy-start.2) | copy-done | bytes 1560
  3.0 0.0 copy-start.3
  3.0 0.7 %copy-done.3 = s32[5]{0:T(128)S(1)} copy-done((s32[5]{0:T(128)S(1)}, s32[5]{0:T(128)}, u32[]{:S(2)}) %copy-start.3) | copy-done | bytes 44
  3.7 0.0 copy-start.4
  3.7 30.3 %step.1 = (f32[6,64,160]{2,1,0:T(8,128)S(1)}, bf16[16,32,128]{2,1,0:T(8,128)(2,1)S(1)}) custom-call(s32[5]{0:T(128)S(1)} %copy-done.3, s32[5120]{0:T(1024)S(1)} %copy-done.1, f32[384]{0:T(512)S(1)} %copy-done.2, f32[6,64,160]{2,1,0:T(8,128)S(1)} %bitcast.12, f32[2,32,32,160]{3,2,1,0:T(8,128)} %bitcast.13, f32[1,32,32,160]{3,2,1,0:T(8,128)} %bitcast.14, ...), custom_call_target="tpu_custom_call" | custom-call | tf_op jit(solution)/shard_map/step/pallas_call | solution.py:560
  34.0 0.0 copy-done.4
  34.0 1.5 %stencil.1 = (f32[6,64,160]{2,1,0:T(8,128)}, f32[6,64,160]{2,1,0:T(8,128)}) custom-call(f32[64]{0:T(128)S(1)} %copy-done.4, bf16[16,32,128]{2,1,0:T(8,128)(2,1)S(1)} %get-tuple-element.6.back, f32[6,64,160]{2,1,0:T(8,128)S(1)} %get-tuple-element.7.solved), custom_call_target="tpu_custom_call" | custom-call | tf_op jit(solution)/shard_map/stencil/pallas_call | solution.py:594
Async XLA Ops:
  0.6 1.0 %copy-start = (f32[3,2,160,64]{2,3,1,0:T(8,128)S(1)}, f32[3,2,160,64]{2,3,1,0:T(8,128)}, u32[]{:S(2)}) copy-start(f32[3,2,160,64]{2,3,1,0:T(8,128)} %param.10) | copy-start | bytes 737284
  1.6 0.7 %copy-start.1 = (s32[5120]{0:T(1024)S(1)}, s32[5120]{0:T(1024)}, u32[]{:S(2)}) copy-start(s32[5120]{0:T(1024)} %slots_hbm.1) | copy-start | bytes 61444
  2.4 0.7 %copy-start.2 = (f32[384]{0:T(512)S(1)}, f32[384]{0:T(512)}, u32[]{:S(2)}) copy-start(f32[384]{0:T(512)} %weight_hbm.1) | copy-start | bytes 4612
  3.0 0.7 %copy-start.3 = (s32[5]{0:T(128)S(1)}, s32[5]{0:T(128)}, u32[]{:S(2)}) copy-start(s32[5]{0:T(128)} %modes_ref.1) | copy-start | bytes 64
  3.7 30.3 %copy-start.4 = (f32[64]{0:T(128)S(1)}, f32[64]{0:T(128)}, u32[]{:S(2)}) copy-start(f32[64]{0:T(128)} %spacing.1) | copy-start | bytes 772

commit v6 on v5

--- a/solution.py
+++ b/solution.py
@@ -94,8 +94,8 @@
 
 def kernel(
     blocks, halves, modes_ref, slots_hbm, weight_hbm, forcing_hbm, pivots_hbm, lower_hbm,
-    upper_hbm, zonal_hbm, legendre_hbm, solved, back,
-    raw_slots, weight, slots, forcing, pivots, lower, upper, zonal, legendre, stage, send, message, hot, spread,
+    upper_hbm, zonal_hbm, legendre_hbm, solved_hbm, back,
+    solved, raw_slots, weight, slots, forcing, pivots, lower, upper, zonal, legendre, stage, send, message, hot, spread,
     waves, spectral, turned, tails, give, other, total, tables,
     load_sem, send_sem, recv_sem, pass_sem, got_sem,
     send2_sem, recv2_sem, pass2_sem, got2_sem,
@@ -248,6 +248,8 @@
         up_step(0, last)
     else:
         lax.fori_loop(0, count - 1, up_step, last)
+    keep = load(9, solved, solved_hbm)
+    keep.start()
     message[lat, me] = send[me]
     to_pair(me, lat).start()
 
@@ -458,6 +460,7 @@
         def _():
             rank_back(rank, me).start()
 
+    keep.wait()
     collect_half(1 - lat, to_other)
     collect_half(lat, to_owner)
     back[me] = total[me]
@@ -561,8 +564,9 @@
         functools.partial(kernel, blocks, halves),
         out_shape=(grid, jax.ShapeDtypeStruct(line, BF16)),
         in_specs=[SMEM] + [HBM] * 8,
-        out_specs=(VMEM, VMEM),
+        out_specs=(HBM, VMEM),
         scratch_shapes=[
+            pltpu.VMEM((items, depth, columns), F32),
             pltpu.VMEM(slot_of_column.shape, jnp.int32),
             pltpu.VMEM(cycle_weight.shape, F32),
             pltpu.VMEM((1, total), jnp.int32),
@@ -582,11 +586,11 @@
             pltpu.VMEM(line, BF16),
             pltpu.VMEM(line, BF16),
             pltpu.VMEM((4 * modes * 8, zonal_flow.shape[2]), BF16),
-            pltpu.SemaphoreType.DMA((9,)),
+            pltpu.SemaphoreType.DMA((10,)),
         ]
         + [pltpu.SemaphoreType.DMA((ranks,))] * 8,
         compiler_params=pltpu.CompilerParams(
-            vmem_limit_bytes=(53 if total <= 8000 else 60) * MIB, collective_id=0, has_side_effects=True
+            vmem_limit_bytes=(54 if total <= 8000 else 60) * MIB, collective_id=0, has_side_effects=True
         ),
         name="step",
     )(slab_modes, slot_of_column, cycle_weight, right, *matrices, zonal_flow, legendre)

time: 35.8 us -> 35.6 us (level)
  local copies, waits for them, and re-layouts: 3.06 us -> 1.9 us
  Pallas kernels: 31.8 us -> 32.8 us
    unnamed x10 -> x6, local copies, waits for them, and re-layouts: 3.06 us -> 1.9 us
    pallas_call x1, Pallas kernels: 30.3 us -> 31.3 us  [body(): pl.pallas_call(functools.partial(kernel, blocks, halves), out_shape=(grid...]
where the time goes in v6:
time: 35.6 us; the launch traced here: 35.4 us
  Pallas kernels  32.8 us (92%)
  local copies, waits for them, and re-layouts  1.9 us (5%)
  between operations  0.67 us (2%)
    pallas_call x1, Pallas kernels, body(): pl.pallas_call(functools.partial(kernel, blocks, halves), out_shape=(grid...  31.3 us
    unnamed x6, local copies, waits for them, and re-layouts  1.9 us
    pallas_call x1, Pallas kernels, body(): pl.pallas_call(functools.partial(last_kernel, blocks), out_shape=(grid, g...  1.53 us

profile of v6, /device:TPU:0, one launch (start us, length us, event | category | flops | bytes accessed | tf_op | source)
XLA Modules:
  0.0 35.4 jit_solution(2151240386545086396)
XLA Ops:
  0.6 0.0 copy-start.2
  0.6 31.3 %step.1 = (f32[6,64,160]{2,1,0:T(8,128)}, bf16[16,32,128]{2,1,0:T(8,128)(2,1)}) custom-call(s32[5]{0:T(128)} %modes_ref.1, s32[5120]{0:T(1024)} %slots_hbm.1, f32[384]{0:T(512)} %weight_hbm.1, f32[6,64,160]{2,1,0:T(8,128)} %bitcast.15, f32[2,32,32,160]{3,2,1,0:T(8,128)} %bitcast.12, f32[1,32,32,160]{3,2,1,0:T(8,128)} %bitcast.13, ...), custom_call_target="tpu_custom_call" | custom-call | tf_op jit(solution)/shard_map/step/pallas_call | solution.py:563
  32.0 0.0 copy-done.2
  32.0 0.0 copy-start
  32.0 1.0 %copy-done = f32[6,64,160]{2,1,0:T(8,128)S(1)} copy-done((f32[6,64,160]{2,1,0:T(8,128)S(1)}, f32[6,64,160]{2,1,0:T(8,128)}, u32[]{:S(2)}) %copy-start) | copy-done | bytes 245784
  33.0 0.0 copy-start.1
  33.0 0.9 %copy-done.1 = bf16[16,32,128]{2,1,0:T(8,128)(2,1)S(1)} copy-done((bf16[16,32,128]{2,1,0:T(8,128)(2,1)S(1)}, bf16[16,32,128]{2,1,0:T(8,128)(2,1)}, u32[]{:S(2)}) %copy-start.1) | copy-done | bytes 131096
  33.9 1.5 %stencil.1 = (f32[6,64,160]{2,1,0:T(8,128)}, f32[6,64,160]{2,1,0:T(8,128)}) custom-call(f32[64]{0:T(128)S(1)} %copy-done.2, bf16[16,32,128]{2,1,0:T(8,128)(2,1)S(1)} %copy-done.1, f32[6,64,160]{2,1,0:T(8,128)S(1)} %copy-done), custom_call_target="tpu_custom_call" | custom-call | tf_op jit(solution)/shard_map/stencil/pallas_call | solution.py:598
Async XLA Ops:
  0.6 31.3 %copy-start.2 = (f32[64]{0:T(128)S(1)}, f32[64]{0:T(128)}, u32[]{:S(2)}) copy-start(f32[64]{0:T(128)} %spacing.1) | copy-start | bytes 772
  32.0 1.0 %copy-start = (f32[6,64,160]{2,1,0:T(8,128)S(1)}, f32[6,64,160]{2,1,0:T(8,128)}, u32[]{:S(2)}) copy-start(f32[6,64,160]{2,1,0:T(8,128)} %get-tuple-element.7.solved) | copy-start | bytes 737284
  33.0 0.9 %copy-start.1 = (bf16[16,32,128]{2,1,0:T(8,128)(2,1)S(1)}, bf16[16,32,128]{2,1,0:T(8,128)(2,1)}, u32[]{:S(2)}) copy-start(bf16[16,32,128]{2,1,0:T(8,128)(2,1)} %get-tuple-element.6.back) | copy-start | bytes 393220
